TPU v7x, 128 devices: a whole 4x4x4 slice. The times are simulated.
128 devices in a mesh: row: 8 (over x, core), col: 16 (over y, z).
Axes of the slice: x: 4, y: 4, z: 4, core: 2. Of those that a mesh axis runs over, the one named last changes fastest.
Arguments:
- modes: float32 [2048, 30720], P('col', 'row'), may hold values from -6 to 6
- prev_modes: float32 [2048, 30720], P('col', 'row'), may hold values from -9 to 9
- first_vectors: float32 [256, 30720], P('col', 'row'), may hold values from -1 to 1, as said below
- first_factor: float32 [256, 256], replicated, may hold values from -0.4 to 0.6, as said below
- second_vectors: float32 [256, 30720], P('col', 'row'), may hold values from -1 to 1, as said below
- second_factor: float32 [256, 256], replicated, may hold values from -0.4 to 0.6, as said below
Outputs:
- moved: float32 [2048, 30720], P('col', 'row')
- correlation: float32 [2048, 2048], P('col', 'row')
Inputs may be any that keep to these rules, and one draw needn't show every extreme that they name: `first_vectors`: zero where the column index is below the row index, one where they are equal. `second_vectors`: zero where the column index is below the row index plus 256, one where it equals it. `first_factor`: upper triangular. `second_factor`: upper triangular.
All inputs are finite; a program needn't handle non-finite values.
Results may differ from a plain program's by a relative error of at most 0.00005.
Values sent between devices are 32-bit elements; how exact they have to be, the bound alone decides.
A program may use at most 128 MiB of HBM per device.

v0:
```python
import jax
import jax.numpy as jnp
from jax import lax
from jax.sharding import PartitionSpec as P

N = 30720


def matmul(left, right):
    return jnp.dot(left, right, precision=lax.Precision.HIGHEST)


def shards(modes, prev_modes, first_vectors, first_factor, second_vectors, second_factor):
    first_full, second_full = (
        lax.all_gather(first_vectors, "col", axis=0, tiled=True),
        lax.all_gather(second_vectors, "col", axis=0, tiled=True),
    )
    second_proj = lax.psum(matmul(second_full, modes.T), "row")
    partly = modes - matmul(matmul(second_factor, second_proj).T, second_full)
    first_proj = lax.psum(matmul(first_full, partly.T), "row")
    moved = partly - matmul(matmul(first_factor, first_proj).T, first_full)
    partials = matmul(moved, lax.all_gather(prev_modes, "col", axis=0, tiled=True).T)
    correlation = lax.psum_scatter(partials, "row", scatter_dimension=1, tiled=True)
    return (moved, correlation / N)


def solution(mesh):
    in_specs = (P("col", "row"), P("col", "row"), P("col", "row"), P(), P("col", "row"), P())
    out_specs = (P("col", "row"), P("col", "row"))
    return jax.shard_map(shards, mesh=mesh, in_specs=in_specs, out_specs=out_specs, check_vma=False)
```

profile of v0, /device:TPU:1, one launch (start us, length us, event | category | flops | bytes accessed | tf_op | source)
XLA Modules:
  0.0 509.6 jit_solution(5983829051140795478)
XLA Ops:
  7.2 0.0 copy-start
  7.2 0.0 all-gather.4.cloned.1.call-start
  7.2 0.7 all-gather.4.cloned.1.call-update
  7.9 0.0 all-reduce.3.cloned.1.call-start
  8.0 56.0 %all-gather.4.cloned.1.call-done = f32[256,3840]{1,0:T(8,128)} async-done(((f32[16,3840]{1,0:T(8,128)}), f32[256,3840]{1,0:T(8,128)}) %all-gather.4.cloned.1.call-update) | async-done | bytes 3932176 | tf_op jit(solution)/shard_map/all_gather | solution.py:16
  63.9 6.6 %fusion = f32[256,128]{1,0:T(8,128)} fusion(f32[256,3840]{1,0:T(8,128)} %all-gather.4.cloned.1.call-done, f32[128,3840]{1,0:T(8,128)} %param.6), kind=kOutput, calls=%fused_computation.4 | convolution fusion | flops 1509949440 | bytes 6029312 | tf_op jit(solution)/shard_map/dot_general | solution.py:10
  70.5 0.0 all-reduce.3.cloned.1.call-update
  70.6 0.0 all-gather.6.cloned.1.call-start
  70.6 0.7 all-gather.6.cloned.1.call-update
  71.3 0.0 all-reduce.5.cloned.1.call-start
  71.3 56.0 %all-reduce.3.cloned.1.call-done = f32[256,128]{1,0:T(8,128)} async-done(((f32[256,128]{1,0:T(8,128)}), f32[256,128]{1,0:T(8,128)}) %all-reduce.3.cloned.1.call-update) | async-done | bytes 131088 | tf_op jit(solution)/shard_map/psum | solution.py:18
  127.4 0.0 copy-done
  127.4 1.3 fusion.1
  128.7 4.9 convolution_subtract_fusion.1
  133.5 47.9 %all-gather.6.cloned.1.call-done = f32[256,3840]{1,0:T(8,128)} async-done(((f32[16,3840]{1,0:T(8,128)}), f32[256,3840]{1,0:T(8,128)}) %all-gather.6.cloned.1.call-update) | async-done | bytes 3932176 | tf_op jit(solution)/shard_map/all_gather | solution.py:15
  181.5 6.8 %convolution_bitcast_fusion = f32[256,128]{0,1:T(8,128)} fusion(f32[128,3840]{1,0:T(8,128)S(1)} %convolution_subtract_fusion.1, f32[256,3840]{1,0:T(8,128)} %all-gather.6.cloned.1.call-done), kind=kOutput, calls=%fused_computation.2 | convolution fusion | flops 1509949440 | bytes 6029312 | tf_op jit(solution)/shard_map/dot_general | solution.py:10
  188.3 0.0 copy-start.1
  188.3 0.0 all-reduce.5.cloned.1.call-update
  188.3 0.0 all-gather.8.cloned.1.call-start
  188.3 0.5 all-gather.8.cloned.1.call-update
  188.9 0.2 reduce-scatter.2.cloned.1.call-start
  189.1 56.0 %all-reduce.5.cloned.1.call-done = f32[256,128]{0,1:T(8,128)} async-done(((f32[256,128]{0,1:T(8,128)}), f32[256,128]{0,1:T(8,128)}) %all-reduce.5.cloned.1.call-update) | async-done | bytes 131088 | tf_op jit(solution)/shard_map/psum | solution.py:20
  245.1 0.0 copy-done.1
  245.1 1.3 fusion.2
  246.4 5.5 %convolution_subtract_fusion = f32[128,3840]{1,0:T(8,128)} fusion(f32[128,3840]{1,0:T(8,128)S(1)} %convolution_subtract_fusion.1, f32[128,256]{1,0:T(8,128)S(1)} %fusion.2, f32[256,3840]{1,0:T(8,128)} %all-gather.6.cloned.1.call-done), kind=kOutput, calls=%fused_computation | convolution fusion | flops 1510440960 | bytes 7995392 | tf_op jit(solution)/shard_map/dot_general | solution.py:10
  251.9 182.9 %all-gather.8.cloned.1.call-done = f32[2048,3840]{1,0:T(8,128)} async-done(((f32[128,3840]{1,0:T(8,128)}), f32[2048,3840]{1,0:T(8,128)}) %all-gather.8.cloned.1.call-update) | async-done | bytes 31457296 | tf_op jit(solution)/shard_map/all_gather | solution.py:22
  434.8 37.5 %fusion.3 = f32[128,2048]{1,0:T(8,128)} fusion(f32[128,3840]{1,0:T(8,128)} %convolution_subtract_fusion, f32[2048,3840]{1,0:T(8,128)} %all-gather.8.cloned.1.call-done), kind=kOutput, calls=%fused_computation.7 | convolution fusion | flops 12079595520 | bytes 34471936 | tf_op jit(solution)/shard_map/dot_general | solution.py:10
  472.3 0.0 reduce-scatter.2.cloned.1.call-update
  472.3 28.9 %reduce-scatter.2.cloned.1.call-done = f32[128,256]{1,0:T(8,128)} async-done(((f32[128,2048]{1,0:T(8,128)}), f32[128,256]{1,0:T(8,128)}) %reduce-scatter.2.cloned.1.call-update) | async-done | bytes 131088 | tf_op jit(solution)/shard_map/reduce_scatter | solution.py:23
  501.2 1.6 broadcast_multiply_fusion
Async XLA Ops:
  7.2 120.2 %copy-start = (f32[256,256]{1,0:T(8,128)S(1)}, f32[256,256]{1,0:T(8,128)}, u32[]{:S(2)}) copy-start(f32[256,256]{1,0:T(8,128)} %param.11) | copy-start | bytes 786436
  7.2 56.8 %all-gather.4.cloned.1.call-start = ((), (), s32[]{:S(2)}) async-start(), calls=%async_computation.1 | async-start | bytes 4177920 | tf_op jit(solution)/shard_map/all_gather | solution.py:16
  7.9 119.4 %all-reduce.3.cloned.1.call-start = ((), (), s32[]{:S(2)}) async-start(), calls=%async_computation.2 | async-start | bytes 262144 | tf_op jit(solution)/shard_map/psum | solution.py:18
  70.6 110.9 %all-gather.6.cloned.1.call-start = ((), (), s32[]{:S(2)}) async-start(), calls=%async_computation.3 | async-start | bytes 4177920 | tf_op jit(solution)/shard_map/all_gather | solution.py:15
  71.3 173.8 %all-reduce.5.cloned.1.call-start = ((), (), s32[]{:S(2)}) async-start(), calls=%async_computation.4 | async-start | bytes 262144 | tf_op jit(solution)/shard_map/psum | solution.py:20
  188.3 56.8 %copy-start.1 = (f32[256,256]{1,0:T(8,128)S(1)}, f32[256,256]{1,0:T(8,128)}, u32[]{:S(2)}) copy-start(f32[256,256]{1,0:T(8,128)} %param.9) | copy-start | bytes 786436
  188.3 246.5 %all-gather.8.cloned.1.call-start = ((), (), s32[]{:S(2)}) async-start(), calls=%async_computation.5 | async-start | bytes 33423360 | tf_op jit(solution)/shard_map/all_gather | solution.py:22
  188.9 312.3 %reduce-scatter.2.cloned.1.call-start = ((), (), s32[]{:S(2)}) async-start(), calls=%async_computation.6 | async-start | bytes 1179648 | tf_op jit(solution)/shard_map/reduce_scatter | solution.py:23
Sparse Core Ops, SparseCore 0:
  10.2 53.6 all-gather.3
  70.7 56.6 all-reduce.2
  129.8 51.6 all-gather.5
  188.4 56.6 all-reduce.4
  247.1 187.6 all-gather.7
  472.5 28.6 reduce-scatter.1
where the time goes:
time: 512 us; the launch traced here: 510 us
  waiting for transfers between devices  430 us (84%)
  matrix products  63.8 us (12%)
  between operations  14.1 us (3%)
    all_gather x1, waiting for transfers between devices, shards(): lax.all_gather(prev_modes, 'col', axis=0, tiled=True)  183 us
    dot_general x7, matrix products, matmul(): return jnp.dot(left, right, precision=lax.Precision.HIGHEST)  63.8 us
    psum x1, waiting for transfers between devices, shards(): second_proj = lax.psum(matmul(second_full, modes.T), 'row')  56 us
    psum x1, waiting for transfers between devices, shards(): first_proj = lax.psum(matmul(first_full, partly.T), 'row')  56 us
    all_gather x1, waiting for transfers between devices, shards(): lax.all_gather(second_vectors, 'col', axis=0, tiled=True)  56 us
    all_gather x1, waiting for transfers between devices, shards(): lax.all_gather(first_vectors, 'col', axis=0, tiled=True)  47.9 us
    reduce_scatter x1, waiting for transfers between devices, shards(): lax.psum_scatter(partials, 'row', scatter_dimension=1, tiled=True)  28.9 us
  transfers between devices with their start and end apart: 6, of which 6 were waited for; matrix products, arithmetic and copies ran while one was open for 3% of the time, Pallas kernels for 0%

commit v1 on v0

v1 whole, which is shorter than its diff:
```python
import functools

import jax
import jax.numpy as jnp
from jax import lax
from jax.experimental import pallas as pl
from jax.experimental.pallas import tpu as pltpu
from jax.sharding import PartitionSpec as P

N = 30720
MESH = pl.DeviceIdType.MESH
F32 = jnp.float32
BF16 = jnp.bfloat16
W = 1024
ODD_FIRST = (1, 3, 2)


def split(value):
    high = value.astype(BF16)
    return high, (value - high.astype(F32)).astype(BF16)


def dot3(left, right, dims):
    (lh, ll), (rh, rl) = left, right
    mul = functools.partial(lax.dot_general, dimension_numbers=(dims, ((), ())), preferred_element_type=F32)
    return mul(lh, rh) + (mul(lh, rl) + mul(ll, rh))


NT = ((1,), (1,))
NN = ((1,), (0,))


class Names:
    def __init__(self):
        self.ids = {}

    def __call__(self, *name):
        return self.ids.setdefault(name, len(self.ids))


def kernel(m_in, p_in, v1_in, v2_in, f1, f2, out_m, out_c,
           mk, pk, vk, mh, ml, vh, vl, ph, plo, at, ac, ax, asum, ay, af, wh, wl,
           ck, cs, cc, cx, cf, cy, ss, rs, ls):
    r, col = lax.axis_index("row"), lax.axis_index("col")
    x, c = lax.div(r, 2), lax.rem(r, 2)
    y, z = lax.div(col, 4), lax.rem(col, 4)
    eight = lax.rem(y + c, 2) == 0

    def wrap(a):
        return lax.rem(a, 4)

    def yid(d):
        return (r, wrap(y + d) * 4 + z)

    def zid(d):
        return (r, y * 4 + wrap(z + d))

    def xid(d):
        return (wrap(x + d) * 2 + c, col)

    other = (x * 2 + 1 - c, col)
    names, local_names = Names(), Names()

    def both(fn):
        @pl.when(eight)
        def _():
            fn(8)

        @pl.when(jnp.logical_not(eight))
        def _():
            fn(7)

    def remote(name, src, dst, dev):
        i = names(*name)
        return pltpu.make_async_remote_copy(
            src_ref=src, dst_ref=dst, send_sem=ss.at[i], recv_sem=rs.at[i], device_id=dev, device_id_type=MESH)

    def quarter(q, n):
        start = 15 * lax.div(q, 2) + lax.rem(q, 2) * (8 - c)
        return pl.ds(pl.multiple_of(start * 128, 128), n * 128)

    def width(n, d):
        return 15 - n if d % 2 else n

    def prow(yy, zz, half=None):
        base = (yy * 4 + zz) * 128
        if half is None:
            return pl.ds(pl.multiple_of(base, 128), 128)
        return pl.ds(pl.multiple_of(base + half * 64, 64), 64)

    def mrow(yy):
        return pl.ds(pl.multiple_of(yy * 128, 128), 128)

    sends = []

    def y_v(n, d, p):
        nd, q = width(n, d), wrap(y + d)
        src = (v1_in, v2_in)[p]
        return remote(("yv", d, p), src.at[:, quarter(q, nd)], vk.at[p, y, z, :, pl.ds(0, nd * 128)], yid(d))

    def y_v_in(n, d, p):
        dst = vk.at[p, wrap(y + 4 - d), z, :, pl.ds(0, n * 128)]
        return remote(("yv", d, p), dst, dst, yid(d))

    def y_m(n, d):
        nd, q = width(n, d), wrap(y + d)
        return remote(("ym", d), m_in.at[:, quarter(q, nd)], mk.at[mrow(y), pl.ds(0, nd * 128)], yid(d))

    def y_m_in(n, d):
        dst = mk.at[mrow(wrap(y + 4 - d)), pl.ds(0, n * 128)]
        return remote(("ym", d), dst, dst, yid(d))

    def y_p(n, d, half):
        nd, q = width(n, d), wrap(y + d)
        return remote(("yp", d, half), p_in.at[pl.ds(half * 64, 64), quarter(q, nd)],
                      pk.at[prow(y, z, half), pl.ds(0, nd * 128)], yid(d))

    def y_p_in(n, d, half):
        dst = pk.at[prow(wrap(y + 4 - d), z, half), pl.ds(0, n * 128)]
        return remote(("yp", d, half), dst, dst, yid(d))

    def z_v(n, s):
        ref = vk.at[:, :, z, :, pl.ds(0, n * 128)]
        return remote(("zv", s), ref, ref, zid(s))

    def z_v_in(n, s):
        ref = vk.at[:, :, wrap(z + 4 - s), :, pl.ds(0, n * 128)]
        return remote(("zv", s), ref, ref, zid(s))

    def z_vf(n, s):
        ref = vk.at[0 if s == 1 else 1, :, wrap(z + 4 - s), :, pl.ds(0, n * 128)]
        return remote(("zvf", s), ref, ref, zid(s))

    def z_vf_in(n, s):
        ref = vk.at[0 if s == 1 else 1, :, wrap(z + 2), :, pl.ds(0, n * 128)]
        return remote(("zvf", s), ref, ref, zid(s))

    def z_p(n, e, s, half):
        ref = pk.at[prow(wrap(y + e), z, half), pl.ds(0, n * 128)]
        src = p_in.at[pl.ds(half * 64, 64), quarter(y, n)] if e == 0 else ref
        return remote(("zp", e, s, half), src, ref, zid(s))

    def z_p_in(n, e, s, half):
        ref = pk.at[prow(wrap(y + e), wrap(z + 4 - s), half), pl.ds(0, n * 128)]
        return remote(("zp", e, s, half), ref, ref, zid(s))

    def z_pf(n, e, s):
        ref = pk.at[prow(wrap(y + e), wrap(z + 4 - s), 0 if s == 1 else 1), pl.ds(0, n * 128)]
        return remote(("zpf", e, s), ref, ref, zid(s))

    def z_pf_in(n, e, s):
        ref = pk.at[prow(wrap(y + e), wrap(z + 2), 0 if s == 1 else 1), pl.ds(0, n * 128)]
        return remote(("zpf", e, s), ref, ref, zid(s))

    def y_r(n, d):
        q = wrap(y + d)
        return remote(("yr", d), mk.at[mrow(q), pl.ds(0, n * 128)], out_m.at[:, quarter(y, n)], yid(d))

    def y_r_in(n, d):
        dst = out_m.at[:, quarter(wrap(y + 4 - d), width(n, d))]
        return remote(("yr", d), dst, dst, yid(d))

    def start(*fns):
        both(lambda n: [f(n).start() for f in fns] and None)
        sends.extend(fns)

    def arrived(*fns):
        both(lambda n: [f(n).wait_recv() for f in fns] and None)

    part = functools.partial

    @pl.when(jnp.logical_not(eight))
    def _():
        mk[:, pl.ds(896, 128)] = jnp.zeros((512, 128), F32)
        pk[:, pl.ds(896, 128)] = jnp.zeros((2048, 128), F32)
        vk[:, :, :, :, pl.ds(896, 128)] = jnp.zeros((2, 4, 4, 16, 128), F32)

    barrier = pltpu.get_barrier_semaphore()
    peers = [yid(1), yid(2), yid(3), zid(1), zid(3), xid(1), xid(2), xid(3), other]
    for dev in peers:
        pl.semaphore_signal(barrier, inc=1, device_id=dev, device_id_type=MESH)
    pl.semaphore_wait(barrier, len(peers))

    start(*[part(y_v, d=d, p=p) for d in ODD_FIRST for p in (0, 1)])
    start(part(z_p, e=0, s=1, half=0), part(z_p, e=0, s=3, half=1))

    def own(n):
        return [
            pltpu.make_async_copy(v1_in.at[:, quarter(y, n)], vk.at[0, y, z, :, pl.ds(0, n * 128)], ls.at[0]),
            pltpu.make_async_copy(v2_in.at[:, quarter(y, n)], vk.at[1, y, z, :, pl.ds(0, n * 128)], ls.at[1]),
            pltpu.make_async_copy(m_in.at[:, quarter(y, n)], mk.at[mrow(y), pl.ds(0, n * 128)], ls.at[2]),
            pltpu.make_async_copy(p_in.at[:, quarter(y, n)], pk.at[prow(y, z), pl.ds(0, n * 128)], ls.at[3]),
        ]

    both(lambda n: [q.start() for q in own(n)] and None)
    start(*[part(y_m, d=d) for d in ODD_FIRST])
    start(*[part(y_p, d=d, half=h) for ds in ((1, 3), (2,)) for h in (0, 1) for d in ds])

    arrived(*[part(y_v_in, d=d, p=p) for d in ODD_FIRST for p in (0, 1)])
    both(lambda n: [q.wait() for q in own(n)] and None)
    start(part(z_v, s=1), part(z_v, s=3))
    start(part(z_p, e=0, s=1, half=1), part(z_p, e=0, s=3, half=0))

    def forward(e):
        arrived(part(z_p_in, e=e, s=1, half=0))
        start(part(z_pf, e=e, s=1))
        arrived(part(z_p_in, e=e, s=3, half=1))
        start(part(z_pf, e=e, s=3))

    def along_z(e, half):
        arrived(part(y_p_in, d=4 - e, half=half))
        order = (1, 3) if half == 0 else (3, 1)
        start(*[part(z_p, e=e, s=s, half=half) for s in order])

    forward(0)
    arrived(part(z_v_in, s=1))
    start(part(z_vf, s=1))
    arrived(part(z_v_in, s=3))
    start(part(z_vf, s=3))

    arrived(*[part(y_m_in, d=d) for d in ODD_FIRST])

    @pl.loop(0, 8)
    def _(i):
        rows = pl.ds(pl.multiple_of(i * 64, 64), 64)
        mh[rows, :], ml[rows, :] = split(mk[rows, :])

    arrived(part(z_vf_in, s=1), part(z_vf_in, s=3))

    @pl.loop(0, 8)
    def _(i):
        p, yy = lax.div(i, 4), lax.rem(i, 4)
        rows = pl.ds(pl.multiple_of(i * 64, 64), 64)
        vh[rows, :], vl[rows, :] = split(vk[p, yy].reshape(64, W))

    @pl.loop(0, 2)
    def _(t):
        rows = pl.ds(pl.multiple_of(t * 256, 256), 256)
        for j in (0, 1):
            cols = pl.ds(j * 256, 256)
            res = dot3((mh[rows, :], ml[rows, :]), (vh[cols, :], vl[cols, :]), NT)
            at[pl.ds(t * 4, 4), pl.ds(0, 64), cols] = res.reshape(4, 64, 256)

    first, second = pl.ds(0, 256), pl.ds(256, 256)
    gram = dot3((vh[first, :], vl[first, :]), (vh[second, :], vl[second, :]), NT)
    at[:, pl.ds(64, 16), first] = gram[:128].reshape(8, 16, 256)
    at[:, pl.ds(64, 16), second] = gram[128:].reshape(8, 16, 256)

    mine, theirs = pl.ds(c * 4, 4), pl.ds((1 - c) * 4, 4)
    fixed = []

    def go(copy):
        copy.start()
        fixed.append(copy)
        return copy

    core_sum = go(remote(("ac",), at.at[theirs], ac, other))
    along_z(1, 0)
    along_z(3, 0)
    core_sum.wait_recv()
    for k in range(4):
        at[c * 4 + k] = at[c * 4 + k] + ac[k]
    x_sum = [go(remote(("ax", d), at.at[c * 4 + wrap(x + d)], ax.at[d - 1], xid(d))) for d in ODD_FIRST]
    along_z(1, 1)
    along_z(3, 1)
    for q in x_sum:
        q.wait_recv()
    asum[...] = (at[c * 4 + x] + ax[0]) + (ax[1] + ax[2])
    y_sum = [go(remote(("ay", d), asum, ay.at[d - 1], yid(d))) for d in ODD_FIRST]
    forward(1)
    along_z(2, 0)
    along_z(2, 1)
    forward(3)
    for q in y_sum:
        q.wait_recv()
    g = c * 4 + x
    af[g] = (asum[...] + ay[0]) + (ay[1] + ay[2])
    x_all = [go(remote(("bx", d), af.at[g], af.at[g], xid(d))) for d in ODD_FIRST]
    for d in ODD_FIRST:
        gd = c * 4 + wrap(x + 4 - d)
        remote(("bx", d), af.at[gd], af.at[gd], xid(d)).wait_recv()
    go(remote(("bc",), af.at[mine], af.at[mine], other))
    remote(("bc",), af.at[theirs], af.at[theirs], other).wait_recv()

    gram = jnp.concatenate([af[:, pl.ds(64, 16), first].reshape(128, 256),
                            af[:, pl.ds(64, 16), second].reshape(128, 256)], axis=0)
    gram2, f1s, f2s = split(gram), split(f1[...]), split(f2[...])
    for t in (0, 1):
        rows = pl.ds(t * 256, 256)
        a1 = af[pl.ds(t * 4, 4), pl.ds(0, 64), first].reshape(256, 256)
        a2 = af[pl.ds(t * 4, 4), pl.ds(0, 64), second].reshape(256, 256)
        w2 = split(dot3(split(a2), f2s, NT))
        wh[rows, second], wl[rows, second] = w2
        w1 = split(dot3(split(a1 - dot3(w2, gram2, NT)), f1s, NT))
        wh[rows, first], wl[rows, first] = w1

    @pl.loop(0, 4)
    def _(j):
        cols = pl.ds(pl.multiple_of(j * 256, 256), 256)
        for t in (0, 1):
            rows = pl.ds(t * 256, 256)
            new = mk[rows, cols] - dot3((wh[rows, :], wl[rows, :]), (vh[:, cols], vl[:, cols]), NN)
            mk[rows, cols] = new
            mh[rows, cols], ml[rows, cols] = split(new)

    start(*[part(y_r, d=d) for d in ODD_FIRST])

    def own_r(n):
        return pltpu.make_async_copy(mk.at[mrow(y), pl.ds(0, n * 128)], out_m.at[:, quarter(y, n)], ls.at[4])

    both(lambda n: own_r(n).start())

    def unit(yy, pair, dst):
        base = pl.multiple_of((yy * 4 + pair * 2) * 128, 256)

        @pl.loop(0, 4)
        def _(i):
            rows = pl.ds(pl.multiple_of(i * 64, 64), 64)
            ph[rows, :], plo[rows, :] = split(pk[pl.ds(pl.multiple_of(base + i * 64, 64), 64), :])

        @pl.loop(0, 2)
        def _(t):
            rows = pl.ds(pl.multiple_of(t * 256, 256), 256)
            dst[yy, rows, :] = dot3((mh[rows, :], ml[rows, :]), (ph[...], plo[...]), NT)

    def to_x(yy, d, wait):
        e = wrap(yy - x + 4)

        @pl.when(e > 0)
        def _():
            i, j = names("cx", d), names("cxr", 1)
            names("cxr", 2), names("cxr", 3)
            copy = pltpu.make_async_remote_copy(
                src_ref=ck.at[yy], dst_ref=cx.at[e - 1], send_sem=ss.at[i], recv_sem=rs.at[j + e - 1],
                device_id=(yy * 2 + c, col), device_id_type=MESH)
            copy.wait_send() if wait else copy.start()

    def reduced(e):
        yy = wrap(y + e)
        remote(("cc", e), cc.at[yy], cc.at[yy], other).wait_recv()

        @pl.loop(0, 4)
        def _(i):
            rows = pl.ds(pl.multiple_of(i * 128, 128), 128)
            ck[yy, rows, :] = ck[yy, rows, :] + cc[yy, rows, :]

        to_x(yy, e, False)

    last = None
    for e in (0, 1, 3, 2):
        yy = wrap(y + e)
        if e == 2:
            forward(2)
        arrived(part(z_p_in, e=e, s=1, half=1), part(z_p_in, e=e, s=3, half=0),
                part(z_pf_in, e=e, s=1), part(z_pf_in, e=e, s=3))
        unit(yy, 1 - c, cs)
        go(remote(("cc", e), cs.at[yy], cc.at[yy], other))
        if last is not None:
            reduced(last)
        unit(yy, c, ck)
        last = e
    reduced(last)

    base = names("cxr", 1)
    for d in range(3):
        pltpu.make_async_remote_copy(
            src_ref=cx.at[d], dst_ref=cx.at[d], send_sem=ss.at[base + d], recv_sem=rs.at[base + d],
            device_id=xid(1), device_id_type=MESH).wait_recv()

    @pl.loop(0, 4)
    def _(i):
        rows = pl.ds(pl.multiple_of(i * 128, 128), 128)
        cf[rows, :] = (ck[x, rows, :] + cx[0, rows, :]) + (cx[1, rows, :] + cx[2, rows, :])

    for d in ODD_FIRST:
        go(remote(("cy", d), cf.at[mrow(wrap(y + d))], cy.at[d - 1], yid(d)))
    for d in ODD_FIRST:
        remote(("cy", d), cf.at[mrow(y)], cy.at[d - 1], yid(d)).wait_recv()
    out_c[...] = ((cf[mrow(y), :] + cy[0]) + (cy[1] + cy[2])) / N

    arrived(*[part(y_r_in, d=d) for d in ODD_FIRST])
    both(lambda n: own_r(n).wait())
    both(lambda n: [f(n).wait_send() for f in sends] and None)
    for copy in fixed:
        copy.wait_send()
    for e in (0, 1, 3, 2):
        to_x(wrap(y + e), e, True)
    assert len(names.ids) <= SEMS


SEMS = 96


def shards(modes, prev_modes, first_vectors, first_factor, second_vectors, second_factor):
    any_, vmem = pl.BlockSpec(memory_space=pl.ANY), pl.BlockSpec(memory_space=pltpu.VMEM)
    V = pltpu.VMEM
    dma = pltpu.SemaphoreType.DMA
    return pl.pallas_call(
        kernel,
        out_shape=(jax.ShapeDtypeStruct((128, 3840), F32), jax.ShapeDtypeStruct((128, 256), F32)),
        in_specs=[any_, any_, any_, any_, vmem, vmem],
        out_specs=(any_, vmem),
        scratch_shapes=[
            V((512, W), F32), V((2048, W), F32), V((2, 4, 4, 16, W), F32),
            V((512, W), BF16), V((512, W), BF16), V((512, W), BF16), V((512, W), BF16),
            V((256, W), BF16), V((256, W), BF16),
            V((8, 80, 512), F32), V((4, 80, 512), F32), V((3, 80, 512), F32), V((80, 512), F32),
            V((3, 80, 512), F32), V((8, 80, 512), F32), V((512, 512), BF16), V((512, 512), BF16),
            V((4, 512, 256), F32), V((4, 512, 256), F32), V((4, 512, 256), F32), V((3, 512, 256), F32),
            V((512, 256), F32), V((3, 128, 256), F32),
            dma((SEMS,)), dma((SEMS,)), dma((5,)),
        ],
        compiler_params=pltpu.CompilerParams(
            collective_id=0, has_side_effects=True, vmem_limit_bytes=56 * 2**20),
        name="reflect_and_correlate",
    )(modes, prev_modes, first_vectors, second_vectors, first_factor, second_factor)


def solution(mesh):
    in_specs = (P("col", "row"), P("col", "row"), P("col", "row"), P(), P("col", "row"), P())
    out_specs = (P("col", "row"), P("col", "row"))
    return jax.shard_map(shards, mesh=mesh, in_specs=in_specs, out_specs=out_specs, check_vma=False)
```

time: 512 us -> 143 us (0.28)
  waiting for transfers between devices: 430 us -> 0 us
  Pallas kernels: 0 us -> 139 us
  matrix products: 63.8 us -> 0 us
  between operations: 14.1 us -> 0.65 us
    all_gather x3 -> x0, waiting for transfers between devices: 287 us -> none  [the longest x1 183 us: shards(): lax.all_gather(prev_modes, 'col', axis=0, tiled=True)]
    pallas_call x0 -> x1, Pallas kernels: none -> 139 us  [shards(): pl.pallas_call(kernel, out_shape=(jax.ShapeDtypeStruct((128, 3840), F32),...]
    psum x2 -> x0, waiting for transfers between devices: 112 us -> none  [the longest x1 56 us: shards(): second_proj = lax.psum(matmul(second_full, modes.T), 'row')]
    dot_general x7 -> x0, matrix products: 63.8 us -> none  [matmul(): return jnp.dot(left, right, precision=lax.Precision.HIGHEST)]
    reduce_scatter x1 -> x0, waiting for transfers between devices: 28.9 us -> none  [shards(): lax.psum_scatter(partials, 'row', scatter_dimension=1, tiled=True)]
  transfers between devices with their start and end apart: 6 -> 0, of which waited for: 6 -> 0; matrix products, arithmetic and copies ran while one was open for 3% -> 0% of each run, Pallas kernels for 0% -> 0%
where the time goes in v1:
time: 143 us
  Pallas kernels  139 us (97%)
  local copies, waits for them, and re-layouts  3.64 us (3%)
    pallas_call x1, Pallas kernels, shards(): pl.pallas_call(kernel, out_shape=(jax.ShapeDtypeStruct((128, 3840), F32),...  139 us
    unnamed x4, local copies, waits for them, and re-layouts  3.64 us

profile of v1, /device:TPU:1, one launch (start us, length us, event | category | flops | bytes accessed | tf_op | source)
XLA Modules:
  0.0 142.9 jit_solution(7578655391892675785)
XLA Ops:
  0.6 138.6 %reflect_and_correlate.1 = (f32[128,3840]{1,0:T(8,128)}, f32[128,256]{1,0:T(8,128)}) custom-call(f32[128,3840]{1,0:T(8,128)} %m_in.1, f32[128,3840]{1,0:T(8,128)} %p_in.1, f32[16,3840]{1,0:T(8,128)} %v1_in.1, f32[16,3840]{1,0:T(8,128)} %v2_in.1, f32[256,256]{1,0:T(8,128)} %f1.1, f32[256,256]{1,0:T(8,128)} %f2.1), custom_call_target="tpu_custom_call" | custom-call | tf_op jit(solution)/shard_map/reflect_and_correlate/pallas_call | solution.py:398
  139.3 0.0 copy-start
  139.3 3.0 %copy.10 = f32[128,3840]{1,0:T(8,128)} copy(f32[128,3840]{1,0:T(8,128)} %get-tuple-element.4) | data formatting | bytes 3932160
  142.2 0.0 copy-done
  142.2 0.7 copy.11
Async XLA Ops:
  139.3 3.0 %copy-start = (f32[128,256]{1,0:T(8,128)S(1)}, f32[128,256]{1,0:T(8,128)}, u32[]{:S(2)}) copy-start(f32[128,256]{1,0:T(8,128)} %get-tuple-element.5) | copy-start | bytes 393220

commit v2 on v0

v2 whole, which is shorter than its diff:
```python
import functools

import jax
import jax.numpy as jnp
from jax import lax
from jax.experimental import pallas as pl
from jax.experimental.pallas import tpu as pltpu
from jax.sharding import PartitionSpec as P

N = 30720
MESH = pl.DeviceIdType.MESH
F32 = jnp.float32
BF16 = jnp.bfloat16
W = 1024
ODD_FIRST = (1, 3, 2)


def split(value):
    high = value.astype(BF16)
    return high, (value - high.astype(F32)).astype(BF16)


def dot3(left, right, dims):
    (lh, ll), (rh, rl) = left, right
    mul = functools.partial(lax.dot_general, dimension_numbers=(dims, ((), ())), preferred_element_type=F32)
    return mul(lh, rh) + (mul(lh, rl) + mul(ll, rh))


NT = ((1,), (1,))
NN = ((1,), (0,))


class Names:
    def __init__(self):
        self.ids = {}

    def __call__(self, *name):
        return self.ids.setdefault(name, len(self.ids))


def kernel(m_in, p_in, v1_in, v2_in, f1, f2, out_m, out_c,
           mk, mp, mv, pk, vk, rh, rl, ph, plo, at, ac, ax, ay, bx_, by_, as_, af, wh, wl,
           ct, cc, cb, kc, kb, cx, bx, sc, sb, fc, fb, dt, cy, of, ss, rs, ls):
    r, col = lax.axis_index("row"), lax.axis_index("col")
    x, c = lax.div(r, 2), lax.rem(r, 2)
    y, z = lax.div(col, 4), lax.rem(col, 4)
    eight = lax.rem(y + c, 2) == 0
    home = c == lax.div(z, 2)
    zl = lax.rem(z, 2)

    def wrap(a):
        return lax.rem(a, 4)

    def yid(d):
        return (r, wrap(y + d) * 4 + z)

    def zid(d):
        return (r, y * 4 + wrap(z + d))

    def xid(d):
        return (wrap(x + d) * 2 + c, col)

    other = (x * 2 + 1 - c, col)
    p_mate = (r, y * 4 + z + 1 - 2 * zl)
    m_mate = (r, y * 4 + 3 - z)
    swap_mate = (x * 2 + 1 - c, y * 4 + 3 - z)
    names = Names()

    def both(fn):
        @pl.when(eight)
        def _():
            fn(8)

        @pl.when(jnp.logical_not(eight))
        def _():
            fn(7)

    def remote(name, src, dst, dev):
        i = names(*name)
        return pltpu.make_async_remote_copy(
            src_ref=src, dst_ref=dst, send_sem=ss.at[i], recv_sem=rs.at[i], device_id=dev, device_id_type=MESH)

    def quarter(q, n):
        start = 15 * lax.div(q, 2) + lax.rem(q, 2) * (8 - c)
        return pl.ds(pl.multiple_of(start * 128, 128), n * 128)

    def width(n, d):
        return 15 - n if d % 2 else n

    def mrow(yy, first=0, count=128):
        return pl.ds(pl.multiple_of(yy * 128 + first, 32), count)

    def lanes(i, step):
        return pl.ds(pl.multiple_of(i * step, step), step)

    sends = []
    fixed = []
    home_sends, away_sends = [], []

    def y_v(n, d, p):
        nd, q = width(n, d), wrap(y + d)
        src = (v1_in, v2_in)[p]
        return remote(("yv", d, p), src.at[:, quarter(q, nd)], vk.at[p, y, z, :, pl.ds(0, nd * 128)], yid(d))

    def y_v_in(n, d, p):
        dst = vk.at[p, wrap(y + 4 - d), z, :, pl.ds(0, n * 128)]
        return remote(("yv", d, p), dst, dst, yid(d))

    def y_m(n, d):
        nd, q = width(n, d), wrap(y + d)
        return remote(("ym", d), m_in.at[:, quarter(q, nd)], mk.at[mrow(y), pl.ds(0, nd * 128)], yid(d))

    def y_m_in(n, d):
        dst = mk.at[mrow(wrap(y + 4 - d)), pl.ds(0, n * 128)]
        return remote(("ym", d), dst, dst, yid(d))

    def y_p(n, d, h):
        nd, q = width(n, d), wrap(y + d)
        return remote(("yp", d, h), p_in.at[h, :, quarter(q, nd)], pk.at[h, 4 - d, zl, :, pl.ds(0, nd * 128)], yid(d))

    def y_p_in(n, d, h):
        dst = pk.at[h, 4 - d, zl, :, pl.ds(0, n * 128)]
        return remote(("yp", d, h), dst, dst, yid(d))

    def z_v(n, s, p):
        ref = vk.at[p, :, z, :, pl.ds(0, n * 128)]
        return remote(("zv", s, p), ref, ref, zid(s))

    def z_v_in(n, s, p):
        ref = vk.at[p, :, wrap(z + 4 - s), :, pl.ds(0, n * 128)]
        return remote(("zv", s, p), ref, ref, zid(s))

    def z_vf(n, s):
        ref = vk.at[0 if s == 1 else 1, :, wrap(z + 4 - s), :, pl.ds(0, n * 128)]
        return remote(("zvf", s), ref, ref, zid(s))

    def z_vf_in(n, s):
        ref = vk.at[0 if s == 1 else 1, :, wrap(z + 2), :, pl.ds(0, n * 128)]
        return remote(("zvf", s), ref, ref, zid(s))

    def z_m0(n, k):
        a, b = ((0, 96), (96, 32))[k]
        return remote(("zm0", k), m_in.at[pl.ds(a, b), quarter(y, n)], mp.at[mrow(y, a, b), pl.ds(0, n * 128)], m_mate)

    def z_m0_in(n, k):
        a, b = ((0, 96), (96, 32))[k]
        ref = mp.at[mrow(y, a, b), pl.ds(0, n * 128)]
        return remote(("zm0", k), ref, ref, m_mate)

    def z_m(n, e):
        rows = mrow(wrap(y + e))
        return remote(("zm", e), mk.at[rows, pl.ds(0, n * 128)], mp.at[rows, pl.ds(0, n * 128)], m_mate)

    def z_p0(n, k):
        a, b = ((0, 3), (3, 1))[k]
        return remote(("zp0", k), p_in.at[pl.ds(a, b), :, quarter(y, n)],
                      pk.at[pl.ds(a, b), 0, zl, :, pl.ds(0, n * 128)], p_mate)

    def z_p0_in(n, k):
        a, b = ((0, 3), (3, 1))[k]
        ref = pk.at[pl.ds(a, b), 0, 1 - zl, :, pl.ds(0, n * 128)]
        return remote(("zp0", k), ref, ref, p_mate)

    def z_p(n, h):
        ref = pk.at[h, pl.ds(1, 3), zl, :, pl.ds(0, n * 128)]
        return remote(("zp", h), ref, ref, p_mate)

    def z_p_in(n, h):
        ref = pk.at[h, pl.ds(1, 3), 1 - zl, :, pl.ds(0, n * 128)]
        return remote(("zp", h), ref, ref, p_mate)

    def y_r(n, d, half):
        return remote(("yr", d, half), mv.at[mrow(wrap(y + d), half * 64, 64), pl.ds(0, n * 128)],
                      out_m.at[pl.ds(half * 64, 64), quarter(y, n)], yid(d))

    def y_r_in(n, d, half):
        dst = out_m.at[pl.ds(half * 64, 64), quarter(wrap(y + 4 - d), width(n, d))]
        return remote(("yr", d, half), dst, dst, yid(d))

    def start(*fns):
        both(lambda n: [f(n).start() for f in fns] and None)
        sends.extend(fns)

    def arrived(*fns):
        both(lambda n: [f(n).wait_recv() for f in fns] and None)

    def go(copy):
        copy.start()
        fixed.append(copy)
        return copy

    part = functools.partial

    @pl.when(jnp.logical_not(eight))
    def _():
        pad = pl.ds(896, 128)
        mk[:, pad] = jnp.zeros((512, 128), F32)
        mp[:, pad] = jnp.zeros((512, 128), F32)
        pk[:, :, :, :, pad] = jnp.zeros((4, 4, 2, 32, 128), F32)
        vk[:, :, :, :, pad] = jnp.zeros((2, 4, 4, 16, 128), F32)

    barrier = pltpu.get_barrier_semaphore()
    peers = [yid(1), yid(2), yid(3), zid(1), zid(3), xid(1), xid(2), xid(3), other, swap_mate]
    for dev in peers:
        pl.semaphore_signal(barrier, inc=1, device_id=dev, device_id_type=MESH)
    pl.semaphore_wait(barrier, len(peers))

    start(*[part(y_v, d=d, p=p) for d in ODD_FIRST for p in (0, 1)])
    start(part(z_p0, k=0), part(z_m0, k=0))

    def own(n):
        return [
            pltpu.make_async_copy(v1_in.at[:, quarter(y, n)], vk.at[0, y, z, :, pl.ds(0, n * 128)], ls.at[0]),
            pltpu.make_async_copy(v2_in.at[:, quarter(y, n)], vk.at[1, y, z, :, pl.ds(0, n * 128)], ls.at[1]),
            pltpu.make_async_copy(m_in.at[:, quarter(y, n)], mk.at[mrow(y), pl.ds(0, n * 128)], ls.at[2]),
            pltpu.make_async_copy(p_in.at[:, :, quarter(y, n)], pk.at[:, 0, zl, :, pl.ds(0, n * 128)], ls.at[3]),
        ]

    both(lambda n: [q.start() for q in own(n)] and None)
    start(*[part(y_m, d=d) for d in ODD_FIRST])

    def y_panel(h):
        start(*[part(y_p, d=d, h=h) for d in ODD_FIRST])

    def z_panel(h):
        arrived(*[part(y_p_in, d=d, h=h) for d in ODD_FIRST])
        start(part(z_p, h=h))

    y_panel(0)
    y_panel(1)

    arrived(*[part(y_v_in, d=d, p=p) for d in ODD_FIRST for p in (0, 1)])
    both(lambda n: [q.wait() for q in own(n)] and None)
    start(part(z_v, s=1, p=0), part(z_v, s=3, p=1), part(z_v, s=1, p=1), part(z_v, s=3, p=0))
    arrived(part(z_v_in, s=1, p=0))
    start(part(z_vf, s=1))
    arrived(part(z_v_in, s=3, p=1))
    start(part(z_vf, s=3))
    start(part(z_p0, k=1), part(z_m0, k=1))
    for e in (1, 3, 2):
        arrived(part(y_m_in, d=4 - e))
        start(part(z_m, e=e))

    @pl.loop(0, 8)
    def _(i):
        rows = pl.ds(pl.multiple_of(i * 64, 64), 64)
        rh[rows, :], rl[rows, :] = split(mk[rows, :])

    arrived(part(z_v_in, s=1, p=1), part(z_v_in, s=3, p=0), part(z_vf_in, s=1), part(z_vf_in, s=3))

    @pl.loop(0, 8)
    def _(i):
        p, yy = lax.div(i, 4), lax.rem(i, 4)
        rows = pl.ds(pl.multiple_of(1024 + i * 64, 64), 64)
        rh[rows, :], rl[rows, :] = split(vk[p, yy].reshape(64, W))

    first, second = pl.ds(0, 256), pl.ds(256, 256)

    @pl.loop(0, 2)
    def _(t):
        rows = pl.ds(pl.multiple_of(t * 256, 256), 256)
        for j, cols in ((0, first), (1, second)):
            vrows = pl.ds(1024 + j * 256, 256)
            res = dot3((rh[rows, :], rl[rows, :]), (rh[vrows, :], rl[vrows, :]), NT)
            at[pl.ds(t * 8, 8), pl.ds(0, 32), cols] = res.reshape(8, 32, 256)

    v1s, v2s = pl.ds(1024, 256), pl.ds(1280, 256)
    gram = dot3((rh[v1s, :], rl[v1s, :]), (rh[v2s, :], rl[v2s, :]), NT)
    at[:, pl.ds(32, 8), first] = gram[:128].reshape(16, 8, 256)
    at[:, pl.ds(32, 8), second] = gram[128:].reshape(16, 8, 256)

    core_sum = go(remote(("ac",), at.at[pl.ds((1 - c) * 8, 8)], ac, other))
    z_panel(0)
    core_sum.wait_recv()
    for k in range(8):
        at[c * 8 + k] = at[c * 8 + k] + ac[k]
    a0, b0 = c * 8, c * 8 + 4
    one = [go(remote(("ax", d), at.at[a0 + wrap(x + d)], ax.at[d - 1], xid(d))) for d in ODD_FIRST]
    one += [go(remote(("by", d), at.at[b0 + wrap(y + d)], by_.at[d - 1], yid(d))) for d in ODD_FIRST]
    y_panel(2)
    z_panel(1)
    for q in one:
        q.wait_recv()
    as_[0] = (at[a0 + x] + ax[0]) + (ax[1] + ax[2])
    as_[1] = (at[b0 + y] + by_[0]) + (by_[1] + by_[2])
    two = [go(remote(("ay", d), as_.at[0], ay.at[d - 1], yid(d))) for d in ODD_FIRST]
    two += [go(remote(("bx", d), as_.at[1], bx_.at[d - 1], xid(d))) for d in ODD_FIRST]
    y_panel(3)

    def product(h, lo, hi):
        @pl.loop(lo, hi)
        def _(t):
            rows = lanes(t, 256)
            ct[h, :, rows] = dot3((ph[h], plo[h]), (rh[rows, :], rl[rows, :]), NT)

    def early(h):
        arrived(part(z_p_in, h=h), *([part(z_p0_in, k=0)] if h == 0 else [part(z_p0_in, k=1)] if h == 3 else []))

        @pl.loop(0, 4)
        def _(e):
            rows = pl.ds(pl.multiple_of(e * 64, 64), 64)
            ph[h, rows, :], plo[h, rows, :] = split(pk[h, e].reshape(64, W))

        product(h, 4, 6)
        go(remote(("cb", h), ct.at[h, :, pl.ds(pl.multiple_of(1024 + (1 - c) * 256, 256), 256)], cb.at[h], other))
        product(h, 0, 2)
        copy = remote(("cc", h), ct.at[h, :, pl.ds(0, 512)], cc.at[h], other)

        @pl.when(jnp.logical_not(home))
        def _():
            copy.start()

        away_sends.append(copy)

    def along_x(name, h, src, dst):
        out = []
        for f in ODD_FIRST:
            e = wrap(x + f - y + 4)
            out.append(remote((name, f, h), src.at[h, pl.ds(pl.multiple_of(e * 64, 64), 64)], dst.at[h, f - 1], xid(f)))
        return out

    def early_x(h):
        remote(("cb", h), cb.at[h], cb.at[h], other).wait_recv()
        kb[h] = ct[h, :, pl.ds(pl.multiple_of(1024 + c * 256, 256), 256)] + cb[h]
        for q in along_x("xb", h, kb, bx):
            go(q)
        copies = along_x("xc", h, kc, cx)

        @pl.when(home)
        def _():
            remote(("cc", h), cc.at[h], cc.at[h], other).wait_recv()
            kc[h] = ct[h, :, pl.ds(0, 512)] + cc[h]
            for q in copies:
                q.start()

        home_sends.extend(copies)

    def late(h):
        product(h, 2, 4)
        copy = remote(("cc", h), ct.at[h, :, pl.ds(512, 512)], cc.at[h], other)

        @pl.when(home)
        def _():
            copy.start()

        home_sends.append(copy)

    def late_x(h):
        copies = along_x("xc", h, kc, cx)

        @pl.when(jnp.logical_not(home))
        def _():
            remote(("cc", h), cc.at[h], cc.at[h], other).wait_recv()
            kc[h] = ct[h, :, pl.ds(512, 512)] + cc[h]
            for q in copies:
                q.start()

        away_sends.extend(copies)

    mine = pl.ds(pl.multiple_of(wrap(x - y + 4) * 64, 64), 64)

    def finish_b(h):
        for f in ODD_FIRST:
            remote(("xb", f, h), bx.at[h, f - 1], bx.at[h, f - 1], xid(f)).wait_recv()
        sb[h] = (kb[h, mine, :] + bx[h, 0]) + (bx[h, 1] + bx[h, 2])
        here = fb.at[h, :, lanes(c, 256)]
        far = remote(("sb2", h), sb.at[h], here, m_mate)
        near, cross = remote(("sb0", h), sb.at[h], here, other), remote(("sb1", h), sb.at[h], here, swap_mate)

        @pl.when(home)
        def _():
            far.start()
            fb[h, :, lanes(c, 256)] = sb[h]

        @pl.when(jnp.logical_not(home))
        def _():
            cross.start()
            near.start()

        home_sends.append(far)
        away_sends.extend([near, cross])

    def finish_c(h):
        for f in ODD_FIRST:
            remote(("xc", f, h), cx.at[h, f - 1], cx.at[h, f - 1], xid(f)).wait_recv()
        total = (kc[h, mine, :] + cx[h, 0]) + (cx[h, 1] + cx[h, 2])
        copy = remote(("sc", h), sc.at[h], fc.at[h], swap_mate)

        @pl.when(home)
        def _():
            fc[h] = total

        @pl.when(jnp.logical_not(home))
        def _():
            sc[h] = total
            copy.start()

        away_sends.append(copy)

    def final(h):
        @pl.when(home)
        def _():
            ref = fb.at[h, :, lanes(1 - c, 256)]
            remote(("sb0", h), ref, ref, other).wait_recv()

        @pl.when(jnp.logical_not(home))
        def _():
            remote(("sc", h), fc.at[h], fc.at[h], swap_mate).wait_recv()
            ref = fb.at[h, :, lanes(1 - c, 256)]
            remote(("sb1", h), ref, ref, swap_mate).wait_recv()
            ref = fb.at[h, :, lanes(c, 256)]
            remote(("sb2", h), ref, ref, m_mate).wait_recv()

        pair = split(fb[h])
        for cols in (first, second):
            dt[h, :, cols] = fc[h, :, cols] - dot3(pair, (wh[cols, :], wl[cols, :]), NT)
        for d in ODD_FIRST:
            go(remote(("cy", d, h), dt.at[h, :, lanes(wrap(y + d), 128)], cy.at[h, d - 1], yid(d)))

    def done(h):
        for d in ODD_FIRST:
            remote(("cy", d, h), cy.at[h, d - 1], cy.at[h, d - 1], yid(d)).wait_recv()
        res = ((dt[h, :, lanes(y, 128)] + cy[h, 0]) + (cy[h, 1] + cy[h, 2])) / N
        of[pl.ds(h * 32, 32), :] = res[:32]
        of[pl.ds(128 + h * 32, 32), :] = res[32:]

    early(0)
    z_panel(2)
    for q in two:
        q.wait_recv()
    af[a0 + x] = (as_[0] + ay[0]) + (ay[1] + ay[2])
    af[b0 + y] = (as_[1] + bx_[0]) + (bx_[1] + bx_[2])
    for d in ODD_FIRST:
        go(remote(("cx", d), af.at[a0 + x], af.at[a0 + x], xid(d)))
        go(remote(("dy", d), af.at[b0 + y], af.at[b0 + y], yid(d)))
    early_x(0)
    early(1)
    z_panel(3)
    for d in ODD_FIRST:
        ref = af.at[a0 + wrap(x + 4 - d)]
        remote(("cx", d), ref, ref, xid(d)).wait_recv()
        ref = af.at[b0 + wrap(y + 4 - d)]
        remote(("dy", d), ref, ref, yid(d)).wait_recv()
    ref = af.at[pl.ds(c * 8, 8)]
    go(remote(("bc",), ref, ref, other))
    early_x(1)
    ref = af.at[pl.ds((1 - c) * 8, 8)]
    remote(("bc",), ref, ref, other).wait_recv()

    gram = jnp.concatenate([af[:, pl.ds(32, 8), first].reshape(128, 256),
                            af[:, pl.ds(32, 8), second].reshape(128, 256)], axis=0)
    gram2, f1s, f2s = split(gram), split(f1[...]), split(f2[...])
    for t in (0, 1):
        rows = pl.ds(t * 256, 256)
        a1 = af[pl.ds(t * 8, 8), pl.ds(0, 32), first].reshape(256, 256)
        a2 = af[pl.ds(t * 8, 8), pl.ds(0, 32), second].reshape(256, 256)
        w2 = split(dot3(split(a2), f2s, NT))
        wh[rows, second], wl[rows, second] = w2
        w1 = split(dot3(split(a1 - dot3(w2, gram2, NT)), f1s, NT))
        wh[rows, first], wl[rows, first] = w1

    vall = pl.ds(1024, 512)

    @pl.loop(0, 4)
    def _(j):
        cols = pl.ds(pl.multiple_of(j * 256, 256), 256)
        for t in (0, 1):
            rows = pl.ds(t * 256, 256)
            mv[rows, cols] = mk[rows, cols] - dot3((wh[rows, :], wl[rows, :]), (rh[vall, cols], rl[vall, cols]), NN)

    start(*[part(y_r, d=d, half=0) for d in ODD_FIRST])

    def own_r(n):
        return pltpu.make_async_copy(mv.at[mrow(y), pl.ds(0, n * 128)], out_m.at[:, quarter(y, n)], ls.at[4])

    both(lambda n: own_r(n).start())

    early(2)
    arrived(part(z_m0_in, k=0), part(z_m0_in, k=1))
    for e in (1, 3, 2):
        rows = mrow(wrap(y + e))
        both(lambda n: remote(("zm", e), mp.at[rows, pl.ds(0, n * 128)], mp.at[rows, pl.ds(0, n * 128)],
                              m_mate).wait_recv())

    @pl.loop(0, 8)
    def _(i):
        rows = pl.ds(pl.multiple_of(i * 64, 64), 64)
        to = pl.ds(pl.multiple_of(512 + i * 64, 64), 64)
        rh[to, :], rl[to, :] = split(mp[rows, :])

    late(0)
    early_x(2)
    late(1)
    late_x(0)
    late(2)
    late_x(1)
    finish_b(0)
    finish_b(1)
    late_x(2)
    early(3)
    late(3)
    start(*[part(y_r, d=d, half=1) for d in ODD_FIRST])
    early_x(3)
    late_x(3)
    finish_c(0)
    finish_c(1)
    finish_b(2)
    final(0)
    finish_c(2)
    final(1)
    finish_b(3)
    finish_c(3)
    final(2)
    final(3)
    for h in range(4):
        done(h)
    out_c[...] = of[...].T

    arrived(*[part(y_r_in, d=d, half=half) for half in (0, 1) for d in ODD_FIRST])
    both(lambda n: own_r(n).wait())
    both(lambda n: [f(n).wait_send() for f in sends] and None)
    for copy in fixed:
        copy.wait_send()

    @pl.when(home)
    def _():
        for copy in home_sends:
            copy.wait_send()

    @pl.when(jnp.logical_not(home))
    def _():
        for copy in away_sends:
            copy.wait_send()

    assert len(names.ids) <= SEMS, len(names.ids)


SEMS = 160


def shards(modes, prev_modes, first_vectors, first_factor, second_vectors, second_factor):
    any_, vmem = pl.BlockSpec(memory_space=pl.ANY), pl.BlockSpec(memory_space=pltpu.VMEM)
    V = pltpu.VMEM
    dma = pltpu.SemaphoreType.DMA
    return pl.pallas_call(
        kernel,
        out_shape=(jax.ShapeDtypeStruct((128, 3840), F32), jax.ShapeDtypeStruct((128, 256), F32)),
        in_specs=[any_, any_, any_, any_, vmem, vmem],
        out_specs=(any_, vmem),
        scratch_shapes=[
            V((512, W), F32), V((512, W), F32), V((512, W), F32), V((4, 4, 2, 32, W), F32), V((2, 4, 4, 16, W), F32),
            V((1536, W), BF16), V((1536, W), BF16), V((4, 256, W), BF16), V((4, 256, W), BF16),
            V((16, 40, 512), F32), V((8, 40, 512), F32), V((3, 40, 512), F32), V((3, 40, 512), F32),
            V((3, 40, 512), F32), V((3, 40, 512), F32), V((2, 40, 512), F32), V((16, 40, 512), F32),
            V((512, 512), BF16), V((512, 512), BF16),
            V((4, 256, 1536), F32), V((4, 256, 512), F32), V((4, 256, 256), F32),
            V((4, 256, 512), F32), V((4, 256, 256), F32), V((4, 3, 64, 512), F32), V((4, 3, 64, 256), F32),
            V((4, 64, 512), F32), V((4, 64, 256), F32), V((4, 64, 512), F32), V((4, 64, 512), F32),
            V((4, 64, 512), F32), V((4, 3, 64, 128), F32), V((256, 128), F32),
            dma((SEMS,)), dma((SEMS,)), dma((5,)),
        ],
        compiler_params=pltpu.CompilerParams(
            collective_id=0, has_side_effects=True, vmem_limit_bytes=60 * 2**20),
        name="reflect_and_correlate",
    )(modes, prev_modes.reshape(4, 32, 3840), first_vectors, second_vectors, first_factor, second_factor)


def solution(mesh):
    in_specs = (P("col", "row"), P("col", "row"), P("col", "row"), P(), P("col", "row"), P())
    out_specs = (P("col", "row"), P("col", "row"))
    return jax.shard_map(shards, mesh=mesh, in_specs=in_specs, out_specs=out_specs, check_vma=False)
```

time: 512 us -> 121 us (0.24)
  waiting for transfers between devices: 430 us -> 0 us
  Pallas kernels: 0 us -> 117 us
  matrix products: 63.8 us -> 0 us
  between operations: 14.1 us -> 0.65 us
    all_gather x3 -> x0, waiting for transfers between devices: 287 us -> none  [the longest x1 183 us: shards(): lax.all_gather(prev_modes, 'col', axis=0, tiled=True)]
    pallas_call x0 -> x1, Pallas kernels: none -> 117 us  [shards(): pl.pallas_call(kernel, out_shape=(jax.ShapeDtypeStruct((128, 3840), F32),...]
    psum x2 -> x0, waiting for transfers between devices: 112 us -> none  [the longest x1 56 us: shards(): second_proj = lax.psum(matmul(second_full, modes.T), 'row')]
    dot_general x7 -> x0, matrix products: 63.8 us -> none  [matmul(): return jnp.dot(left, right, precision=lax.Precision.HIGHEST)]
    reduce_scatter x1 -> x0, waiting for transfers between devices: 28.9 us -> none  [shards(): lax.psum_scatter(partials, 'row', scatter_dimension=1, tiled=True)]
  transfers between devices with their start and end apart: 6 -> 0, of which waited for: 6 -> 0; matrix products, arithmetic and copies ran while one was open for 3% -> 0% of each run, Pallas kernels for 0% -> 0%
where the time goes in v2:
time: 121 us
  Pallas kernels  117 us (97%)
  local copies, waits for them, and re-layouts  3.64 us (3%)
    pallas_call x1, Pallas kernels, shards(): pl.pallas_call(kernel, out_shape=(jax.ShapeDtypeStruct((128, 3840), F32),...  117 us
    unnamed x4, local copies, waits for them, and re-layouts  3.64 us

profile of v2, /device:TPU:1, one launch (start us, length us, event | category | flops | bytes accessed | tf_op | source)
XLA Modules:
  0.0 120.8 jit_solution(14622675077203169622)
XLA Ops:
  0.6 116.5 %reflect_and_correlate.1 = (f32[128,3840]{1,0:T(8,128)}, f32[128,256]{1,0:T(8,128)}) custom-call(f32[128,3840]{1,0:T(8,128)} %m_in.1, f32[4,32,3840]{2,1,0:T(8,128)} %bitcast.1, f32[16,3840]{1,0:T(8,128)} %v1_in.1, f32[16,3840]{1,0:T(8,128)} %v2_in.1, f32[256,256]{1,0:T(8,128)} %f1.1, f32[256,256]{1,0:T(8,128)} %f2.1), custom_call_target="tpu_custom_call" | custom-call | tf_op jit(solution)/shard_map/reflect_and_correlate/pallas_call | solution.py:545
  117.2 0.0 copy-start
  117.2 3.0 %copy.10 = f32[128,3840]{1,0:T(8,128)} copy(f32[128,3840]{1,0:T(8,128)} %get-tuple-element.4) | data formatting | bytes 3932160
  120.1 0.0 copy-done
  120.2 0.7 copy.11
Async XLA Ops:
  117.2 3.0 %copy-start = (f32[128,256]{1,0:T(8,128)S(1)}, f32[128,256]{1,0:T(8,128)}, u32[]{:S(2)}) copy-start(f32[128,256]{1,0:T(8,128)} %get-tuple-element.5) | copy-start | bytes 393220

commit v3 on v2

--- a/solution.py
+++ b/solution.py
@@ -40,7 +40,7 @@
 
 def kernel(m_in, p_in, v1_in, v2_in, f1, f2, out_m, out_c,
            mk, mp, mv, pk, vk, rh, rl, ph, plo, at, ac, ax, ay, bx_, by_, as_, af, wh, wl,
-           ct, cc, cb, kc, kb, cx, bx, sc, sb, fc, fb, dt, cy, of, ss, rs, ls):
+           ct, bt, cc, cb, kc, kb, cx, bx, sc, sb, fc, fb, dt, cy, of, ss, rs, ls):
     r, col = lax.axis_index("row"), lax.axis_index("col")
     x, c = lax.div(r, 2), lax.rem(r, 2)
     y, z = lax.div(col, 4), lax.rem(col, 4)
@@ -165,6 +165,14 @@
         ref = pk.at[h, pl.ds(1, 3), zl, :, pl.ds(0, n * 128)]
         return remote(("zp", h), ref, ref, p_mate)
 
+    def z_pe(n, e, h):
+        ref = pk.at[h, e, zl, :, pl.ds(0, n * 128)]
+        return remote(("zpe", e, h), ref, ref, p_mate)
+
+    def z_pe_in(n, e, h):
+        ref = pk.at[h, e, 1 - zl, :, pl.ds(0, n * 128)]
+        return remote(("zpe", e, h), ref, ref, p_mate)
+
     def z_p_in(n, h):
         ref = pk.at[h, pl.ds(1, 3), 1 - zl, :, pl.ds(0, n * 128)]
         return remote(("zp", h), ref, ref, p_mate)
@@ -190,6 +198,25 @@
         return copy
 
     part = functools.partial
+
+    def drain():
+        widths, plain, here, there = list(sends), list(fixed), list(home_sends), list(away_sends)
+        both(lambda n: [f(n).wait_send() for f in widths] and None)
+        for copy in plain:
+            copy.wait_send()
+
+        @pl.when(home)
+        def _():
+            for copy in here:
+                copy.wait_send()
+
+        @pl.when(jnp.logical_not(home))
+        def _():
+            for copy in there:
+                copy.wait_send()
+
+        for held in (sends, fixed, home_sends, away_sends):
+            held.clear()
 
     @pl.when(jnp.logical_not(eight))
     def _():
@@ -200,7 +227,8 @@
         vk[:, :, :, :, pad] = jnp.zeros((2, 4, 4, 16, 128), F32)
 
     barrier = pltpu.get_barrier_semaphore()
-    peers = [yid(1), yid(2), yid(3), zid(1), zid(3), xid(1), xid(2), xid(3), other, swap_mate]
+    peers = [yid(1), yid(2), yid(3), xid(1), xid(2), xid(3), other, zid(1), zid(2), zid(3)]
+    peers += [(x * 2 + 1 - c, y * 4 + wrap(z + d)) for d in (1, 2, 3)]
     for dev in peers:
         pl.semaphore_signal(barrier, inc=1, device_id=dev, device_id_type=MESH)
     pl.semaphore_wait(barrier, len(peers))
@@ -256,9 +284,8 @@
 
     first, second = pl.ds(0, 256), pl.ds(256, 256)
 
-    @pl.loop(0, 2)
-    def _(t):
-        rows = pl.ds(pl.multiple_of(t * 256, 256), 256)
+    for t in (0, 1):
+        rows = pl.ds(t * 256, 256)
         for j, cols in ((0, first), (1, second)):
             vrows = pl.ds(1024 + j * 256, 256)
             res = dot3((rh[rows, :], rl[rows, :]), (rh[vrows, :], rl[vrows, :]), NT)
@@ -285,24 +312,25 @@
     as_[1] = (at[b0 + y] + by_[0]) + (by_[1] + by_[2])
     two = [go(remote(("ay", d), as_.at[0], ay.at[d - 1], yid(d))) for d in ODD_FIRST]
     two += [go(remote(("bx", d), as_.at[1], bx_.at[d - 1], xid(d))) for d in ODD_FIRST]
-    y_panel(3)
 
     def product(h, lo, hi):
-        @pl.loop(lo, hi)
-        def _(t):
-            rows = lanes(t, 256)
+        for t in range(lo, hi):
+            rows = pl.ds(t * 256, 256)
             ct[h, :, rows] = dot3((ph[h], plo[h]), (rh[rows, :], rl[rows, :]), NT)
 
-    def early(h):
-        arrived(part(z_p_in, h=h), *([part(z_p0_in, k=0)] if h == 0 else [part(z_p0_in, k=1)] if h == 3 else []))
+    def landed(h):
+        arrived(*([part(z_pe_in, e=e, h=h) for e in (1, 3, 2)] if h == 3 else [part(z_p_in, h=h)]),
+                *([part(z_p0_in, k=0)] if h == 0 else [part(z_p0_in, k=1)] if h == 3 else []))
 
         @pl.loop(0, 4)
         def _(e):
             rows = pl.ds(pl.multiple_of(e * 64, 64), 64)
             ph[h, rows, :], plo[h, rows, :] = split(pk[h, e].reshape(64, W))
 
-        product(h, 4, 6)
-        go(remote(("cb", h), ct.at[h, :, pl.ds(pl.multiple_of(1024 + (1 - c) * 256, 256), 256)], cb.at[h], other))
+    def early(h):
+        panel = pl.ds(pl.multiple_of(1024 + zl * 256, 256), 256)
+        bt[h] = dot3((ph[h], plo[h]), (rh[panel, :], rl[panel, :]), NT)
+        go(remote(("cb", h), bt.at[h, :, lanes(1 - c, 128)], cb.at[h], other))
         product(h, 0, 2)
         copy = remote(("cc", h), ct.at[h, :, pl.ds(0, 512)], cc.at[h], other)
 
@@ -321,7 +349,7 @@
 
     def early_x(h):
         remote(("cb", h), cb.at[h], cb.at[h], other).wait_recv()
-        kb[h] = ct[h, :, pl.ds(pl.multiple_of(1024 + c * 256, 256), 256)] + cb[h]
+        kb[h] = bt[h, :, lanes(c, 128)] + cb[h]
         for q in along_x("xb", h, kb, bx):
             go(q)
         copies = along_x("xc", h, kc, cx)
@@ -359,26 +387,35 @@
 
     mine = pl.ds(pl.multiple_of(wrap(x - y + 4) * 64, 64), 64)
 
+    pair = lax.div(z, 2)
+    b_slot = zl * 2 + c
+
+    def b_copies(h):
+        base = names("sbr", h, 0)
+        for k in (1, 2, 3):
+            names("sbr", h, k)
+        return [pltpu.make_async_remote_copy(
+            src_ref=sb.at[h], dst_ref=fb.at[h, :, lanes(b_slot, 128)], send_sem=ss.at[names("sbs", h, k)],
+            recv_sem=rs.at[base + b_slot], device_id=(x * 2 + pair, y * 4 + wrap(z + k)), device_id_type=MESH)
+            for k in range(4)]
+
     def finish_b(h):
         for f in ODD_FIRST:
             remote(("xb", f, h), bx.at[h, f - 1], bx.at[h, f - 1], xid(f)).wait_recv()
         sb[h] = (kb[h, mine, :] + bx[h, 0]) + (bx[h, 1] + bx[h, 2])
-        here = fb.at[h, :, lanes(c, 256)]
-        far = remote(("sb2", h), sb.at[h], here, m_mate)
-        near, cross = remote(("sb0", h), sb.at[h], here, other), remote(("sb1", h), sb.at[h], here, swap_mate)
+        copies = b_copies(h)
+        for q in copies[1:]:
+            go(q)
 
         @pl.when(home)
         def _():
-            far.start()
-            fb[h, :, lanes(c, 256)] = sb[h]
+            fb[h, :, lanes(b_slot, 128)] = sb[h]
 
         @pl.when(jnp.logical_not(home))
         def _():
-            cross.start()
-            near.start()
-
-        home_sends.append(far)
-        away_sends.extend([near, cross])
+            copies[0].start()
+
+        away_sends.append(copies[0])
 
     def finish_c(h):
         for f in ODD_FIRST:
@@ -398,22 +435,19 @@
         away_sends.append(copy)
 
     def final(h):
-        @pl.when(home)
-        def _():
-            ref = fb.at[h, :, lanes(1 - c, 256)]
-            remote(("sb0", h), ref, ref, other).wait_recv()
+        for k in range(4):
+            @pl.when(jnp.logical_not(jnp.logical_and(home, b_slot == k)))
+            def _():
+                ref = fb.at[h, :, pl.ds(k * 128, 128)]
+                remote(("sbr", h, k), ref, ref, other).wait_recv()
 
         @pl.when(jnp.logical_not(home))
         def _():
             remote(("sc", h), fc.at[h], fc.at[h], swap_mate).wait_recv()
-            ref = fb.at[h, :, lanes(1 - c, 256)]
-            remote(("sb1", h), ref, ref, swap_mate).wait_recv()
-            ref = fb.at[h, :, lanes(c, 256)]
-            remote(("sb2", h), ref, ref, m_mate).wait_recv()
-
-        pair = split(fb[h])
+
+        fbs = split(fb[h])
         for cols in (first, second):
-            dt[h, :, cols] = fc[h, :, cols] - dot3(pair, (wh[cols, :], wl[cols, :]), NT)
+            dt[h, :, cols] = fc[h, :, cols] - dot3(fbs, (wh[cols, :], wl[cols, :]), NT)
         for d in ODD_FIRST:
             go(remote(("cy", d, h), dt.at[h, :, lanes(wrap(y + d), 128)], cy.at[h, d - 1], yid(d)))
 
@@ -424,7 +458,9 @@
         of[pl.ds(h * 32, 32), :] = res[:32]
         of[pl.ds(128 + h * 32, 32), :] = res[32:]
 
+    landed(0)
     early(0)
+    early_x(0)
     z_panel(2)
     for q in two:
         q.wait_recv()
@@ -433,9 +469,10 @@
     for d in ODD_FIRST:
         go(remote(("cx", d), af.at[a0 + x], af.at[a0 + x], xid(d)))
         go(remote(("dy", d), af.at[b0 + y], af.at[b0 + y], yid(d)))
-    early_x(0)
+    y_panel(3)
+    landed(1)
     early(1)
-    z_panel(3)
+    early_x(1)
     for d in ODD_FIRST:
         ref = af.at[a0 + wrap(x + 4 - d)]
         remote(("cx", d), ref, ref, xid(d)).wait_recv()
@@ -443,9 +480,19 @@
         remote(("dy", d), ref, ref, yid(d)).wait_recv()
     ref = af.at[pl.ds(c * 8, 8)]
     go(remote(("bc",), ref, ref, other))
-    early_x(1)
+    landed(2)
+    early(2)
     ref = af.at[pl.ds((1 - c) * 8, 8)]
     remote(("bc",), ref, ref, other).wait_recv()
+
+
+    early_x(2)
+
+    def z_last(*es):
+        arrived(*[part(y_p_in, d=4 - e, h=3) for e in es])
+        start(*[part(z_pe, e=e, h=3) for e in es])
+
+    z_last(1, 3)
 
     gram = jnp.concatenate([af[:, pl.ds(32, 8), first].reshape(128, 256),
                             af[:, pl.ds(32, 8), second].reshape(128, 256)], axis=0)
@@ -461,47 +508,52 @@
 
     vall = pl.ds(1024, 512)
 
-    @pl.loop(0, 4)
-    def _(j):
-        cols = pl.ds(pl.multiple_of(j * 256, 256), 256)
-        for t in (0, 1):
-            rows = pl.ds(t * 256, 256)
+    def move(d):
+        rows = mrow(wrap(y + d))
+        for k in range(2):
+            cols = pl.ds(k * 512, 512)
             mv[rows, cols] = mk[rows, cols] - dot3((wh[rows, :], wl[rows, :]), (rh[vall, cols], rl[vall, cols]), NN)
-
-    start(*[part(y_r, d=d, half=0) for d in ODD_FIRST])
 
     def own_r(n):
         return pltpu.make_async_copy(mv.at[mrow(y), pl.ds(0, n * 128)], out_m.at[:, quarter(y, n)], ls.at[4])
 
+    def modes_landed():
+        arrived(part(z_m0_in, k=0), part(z_m0_in, k=1))
+        for e in (1, 3, 2):
+            rows = mrow(wrap(y + e))
+            both(lambda n: remote(("zm", e), mp.at[rows, pl.ds(0, n * 128)], mp.at[rows, pl.ds(0, n * 128)],
+                                  m_mate).wait_recv())
+
+        @pl.loop(0, 8)
+        def _(i):
+            rows = pl.ds(pl.multiple_of(i * 64, 64), 64)
+            to = pl.ds(pl.multiple_of(512 + i * 64, 64), 64)
+            rh[to, :], rl[to, :] = split(mp[rows, :])
+
+    move(1)
+    start(part(y_r, d=1, half=0))
+    move(3)
+    start(part(y_r, d=3, half=0))
+    z_last(2)
+    modes_landed()
+    late(0)
+    move(2)
+    start(part(y_r, d=2, half=0))
+    late_x(0)
+    move(0)
     both(lambda n: own_r(n).start())
-
-    early(2)
-    arrived(part(z_m0_in, k=0), part(z_m0_in, k=1))
-    for e in (1, 3, 2):
-        rows = mrow(wrap(y + e))
-        both(lambda n: remote(("zm", e), mp.at[rows, pl.ds(0, n * 128)], mp.at[rows, pl.ds(0, n * 128)],
-                              m_mate).wait_recv())
-
-    @pl.loop(0, 8)
-    def _(i):
-        rows = pl.ds(pl.multiple_of(i * 64, 64), 64)
-        to = pl.ds(pl.multiple_of(512 + i * 64, 64), 64)
-        rh[to, :], rl[to, :] = split(mp[rows, :])
-
-    late(0)
-    early_x(2)
     late(1)
-    late_x(0)
     late(2)
     late_x(1)
+    late_x(2)
+    start(*[part(y_r, d=d, half=1) for d in ODD_FIRST])
     finish_b(0)
     finish_b(1)
-    late_x(2)
+    landed(3)
+    late(3)
     early(3)
-    late(3)
-    start(*[part(y_r, d=d, half=1) for d in ODD_FIRST])
+    late_x(3)
     early_x(3)
-    late_x(3)
     finish_c(0)
     finish_c(1)
     finish_b(2)
@@ -511,31 +563,20 @@
     finish_b(3)
     finish_c(3)
     final(2)
+    done(0)
+    done(1)
     final(3)
-    for h in range(4):
-        done(h)
+    drain()
+    done(2)
+    done(3)
     out_c[...] = of[...].T
 
     arrived(*[part(y_r_in, d=d, half=half) for half in (0, 1) for d in ODD_FIRST])
     both(lambda n: own_r(n).wait())
-    both(lambda n: [f(n).wait_send() for f in sends] and None)
-    for copy in fixed:
-        copy.wait_send()
-
-    @pl.when(home)
-    def _():
-        for copy in home_sends:
-            copy.wait_send()
-
-    @pl.when(jnp.logical_not(home))
-    def _():
-        for copy in away_sends:
-            copy.wait_send()
-
     assert len(names.ids) <= SEMS, len(names.ids)
 
 
-SEMS = 160
+SEMS = 192
 
 
 def shards(modes, prev_modes, first_vectors, first_factor, second_vectors, second_factor):
@@ -553,9 +594,9 @@
             V((16, 40, 512), F32), V((8, 40, 512), F32), V((3, 40, 512), F32), V((3, 40, 512), F32),
             V((3, 40, 512), F32), V((3, 40, 512), F32), V((2, 40, 512), F32), V((16, 40, 512), F32),
             V((512, 512), BF16), V((512, 512), BF16),
-            V((4, 256, 1536), F32), V((4, 256, 512), F32), V((4, 256, 256), F32),
-            V((4, 256, 512), F32), V((4, 256, 256), F32), V((4, 3, 64, 512), F32), V((4, 3, 64, 256), F32),
-            V((4, 64, 512), F32), V((4, 64, 256), F32), V((4, 64, 512), F32), V((4, 64, 512), F32),
+            V((4, 256, 1024), F32), V((4, 256, 256), F32), V((4, 256, 512), F32), V((4, 256, 128), F32),
+            V((4, 256, 512), F32), V((4, 256, 128), F32), V((4, 3, 64, 512), F32), V((4, 3, 64, 128), F32),
+            V((4, 64, 512), F32), V((4, 64, 128), F32), V((4, 64, 512), F32), V((4, 64, 512), F32),
             V((4, 64, 512), F32), V((4, 3, 64, 128), F32), V((256, 128), F32),
             dma((SEMS,)), dma((SEMS,)), dma((5,)),
         ],

time: 121 us -> 115 us (0.950)
  Pallas kernels: 117 us -> 110 us
    pallas_call x1, Pallas kernels: 117 us -> 110 us  [shards(): pl.pallas_call(kernel, out_shape=(jax.ShapeDtypeStruct((128, 3840), F32),...]
where the time goes in v3:
time: 115 us
  Pallas kernels  110 us (96%)
  local copies, waits for them, and re-layouts  3.64 us (3%)
    pallas_call x1, Pallas kernels, shards(): pl.pallas_call(kernel, out_shape=(jax.ShapeDtypeStruct((128, 3840), F32),...  110 us
    unnamed x4, local copies, waits for them, and re-layouts  3.64 us

profile of v3, /device:TPU:1, one launch (start us, length us, event | category | flops | bytes accessed | tf_op | source)
XLA Modules:
  0.0 114.6 jit_solution(1918388425044655730)
XLA Ops:
  0.6 110.3 %reflect_and_correlate.1 = (f32[128,3840]{1,0:T(8,128)}, f32[128,256]{1,0:T(8,128)}) custom-call(f32[128,3840]{1,0:T(8,128)} %m_in.1, f32[4,32,3840]{2,1,0:T(8,128)} %bitcast.1, f32[16,3840]{1,0:T(8,128)} %v1_in.1, f32[16,3840]{1,0:T(8,128)} %v2_in.1, f32[256,256]{1,0:T(8,128)} %f1.1, f32[256,256]{1,0:T(8,128)} %f2.1), custom_call_target="tpu_custom_call" | custom-call | tf_op jit(solution)/shard_map/reflect_and_correlate/pallas_call | solution.py:586
  110.9 0.0 copy-start
  110.9 3.0 %copy.10 = f32[128,3840]{1,0:T(8,128)} copy(f32[128,3840]{1,0:T(8,128)} %get-tuple-element.4) | data formatting | bytes 3932160
  113.9 0.0 copy-done
  113.9 0.7 copy.11
Async XLA Ops:
  110.9 3.0 %copy-start = (f32[128,256]{1,0:T(8,128)S(1)}, f32[128,256]{1,0:T(8,128)}, u32[]{:S(2)}) copy-start(f32[128,256]{1,0:T(8,128)} %get-tuple-element.5) | copy-start | bytes 393220

commit v4 on v3

--- a/solution.py
+++ b/solution.py
@@ -122,21 +122,21 @@
         dst = pk.at[h, 4 - d, zl, :, pl.ds(0, n * 128)]
         return remote(("yp", d, h), dst, dst, yid(d))
 
-    def z_v(n, s, p):
+    def z_v(n, to, p):
         ref = vk.at[p, :, z, :, pl.ds(0, n * 128)]
-        return remote(("zv", s, p), ref, ref, zid(s))
-
-    def z_v_in(n, s, p):
-        ref = vk.at[p, :, wrap(z + 4 - s), :, pl.ds(0, n * 128)]
-        return remote(("zv", s, p), ref, ref, zid(s))
-
-    def z_vf(n, s):
-        ref = vk.at[0 if s == 1 else 1, :, wrap(z + 4 - s), :, pl.ds(0, n * 128)]
-        return remote(("zvf", s), ref, ref, zid(s))
-
-    def z_vf_in(n, s):
-        ref = vk.at[0 if s == 1 else 1, :, wrap(z + 2), :, pl.ds(0, n * 128)]
-        return remote(("zvf", s), ref, ref, zid(s))
+        return remote(("zv", to, p), ref, ref, p_mate if to == "p" else m_mate)
+
+    def z_v_in(n, to, p):
+        ref = vk.at[p, :, (z + 1 - 2 * zl) if to == "p" else 3 - z, :, pl.ds(0, n * 128)]
+        return remote(("zv", to, p), ref, ref, p_mate)
+
+    def z_vf(n, p):
+        ref = vk.at[p, :, 3 - z, :, pl.ds(0, n * 128)]
+        return remote(("zvf", p), ref, ref, p_mate)
+
+    def z_vf_in(n, p):
+        ref = vk.at[p, :, wrap(z + 2), :, pl.ds(0, n * 128)]
+        return remote(("zvf", p), ref, ref, p_mate)
 
     def z_m0(n, k):
         a, b = ((0, 96), (96, 32))[k]
@@ -245,36 +245,194 @@
         ]
 
     both(lambda n: [q.start() for q in own(n)] and None)
-    start(*[part(y_m, d=d) for d in ODD_FIRST])
-
-    def y_panel(h):
-        start(*[part(y_p, d=d, h=h) for d in ODD_FIRST])
+
+    def y_panel(h, ds=ODD_FIRST):
+        start(*[part(y_p, d=d, h=h) for d in ds])
 
     def z_panel(h):
         arrived(*[part(y_p_in, d=d, h=h) for d in ODD_FIRST])
         start(part(z_p, h=h))
 
+    start(*[part(y_m, d=d) for d in ODD_FIRST])
     y_panel(0)
     y_panel(1)
 
     arrived(*[part(y_v_in, d=d, p=p) for d in ODD_FIRST for p in (0, 1)])
     both(lambda n: [q.wait() for q in own(n)] and None)
-    start(part(z_v, s=1, p=0), part(z_v, s=3, p=1), part(z_v, s=1, p=1), part(z_v, s=3, p=0))
-    arrived(part(z_v_in, s=1, p=0))
-    start(part(z_vf, s=1))
-    arrived(part(z_v_in, s=3, p=1))
-    start(part(z_vf, s=3))
-    start(part(z_p0, k=1), part(z_m0, k=1))
+    start(*[part(z_v, to=to, p=p) for p in (0, 1) for to in "mp"])
+    start(part(z_m0, k=1))
+    for p in (0, 1):
+        arrived(part(z_v_in, to="m", p=p))
+        start(part(z_vf, p=p))
+    start(part(z_p0, k=1))
+
+    first, second = pl.ds(0, 256), pl.ds(256, 256)
+
+    def split_block(src, yy, base):
+        @pl.loop(0, 2)
+        def _(i):
+            start_row = yy * 128 + i * 64
+            to = pl.ds(pl.multiple_of(base + start_row, 64), 64)
+            rh[to, :], rl[to, :] = split(src[pl.ds(pl.multiple_of(start_row, 64), 64), :])
+
+    def product(h, lo, hi):
+        for t in range(lo, hi):
+            rows = pl.ds(t * 256, 256)
+            ct[h, :, rows] = dot3((ph[h], plo[h]), (rh[rows, :], rl[rows, :]), NT)
+
+    def landed(h):
+        arrived(*([part(z_pe_in, e=e, h=h) for e in (1, 3, 2)] if h == 3 else [part(z_p_in, h=h)]),
+                *([part(z_p0_in, k=0)] if h == 0 else [part(z_p0_in, k=1)] if h == 3 else []))
+
+        @pl.loop(0, 4)
+        def _(e):
+            rows = pl.ds(pl.multiple_of(e * 64, 64), 64)
+            ph[h, rows, :], plo[h, rows, :] = split(pk[h, e].reshape(64, W))
+
+    def early(h):
+        panel = pl.ds(pl.multiple_of(1024 + zl * 256, 256), 256)
+        bt[h] = dot3((ph[h], plo[h]), (rh[panel, :], rl[panel, :]), NT)
+        go(remote(("cb", h), bt.at[h, :, lanes(1 - c, 128)], cb.at[h], other))
+        product(h, 0, 2)
+        copy = remote(("cc", h), ct.at[h, :, pl.ds(0, 512)], cc.at[h], other)
+
+        @pl.when(jnp.logical_not(home))
+        def _():
+            copy.start()
+
+        away_sends.append(copy)
+
+    def along_x(name, h, src, dst):
+        out = []
+        for f in ODD_FIRST:
+            e = wrap(x + f - y + 4)
+            out.append(remote((name, f, h), src.at[h, pl.ds(pl.multiple_of(e * 64, 64), 64)], dst.at[h, f - 1], xid(f)))
+        return out
+
+    def early_x(h):
+        remote(("cb", h), cb.at[h], cb.at[h], other).wait_recv()
+        kb[h] = bt[h, :, lanes(c, 128)] + cb[h]
+        for q in along_x("xb", h, kb, bx):
+            go(q)
+        copies = along_x("xc", h, kc, cx)
+
+        @pl.when(home)
+        def _():
+            remote(("cc", h), cc.at[h], cc.at[h], other).wait_recv()
+            kc[h] = ct[h, :, pl.ds(0, 512)] + cc[h]
+            for q in copies:
+                q.start()
+
+        home_sends.extend(copies)
+
+    def late(h):
+        product(h, 2, 4)
+        copy = remote(("cc", h), ct.at[h, :, pl.ds(512, 512)], cc.at[h], other)
+
+        @pl.when(home)
+        def _():
+            copy.start()
+
+        home_sends.append(copy)
+
+    def late_x(h):
+        copies = along_x("xc", h, kc, cx)
+
+        @pl.when(jnp.logical_not(home))
+        def _():
+            remote(("cc", h), cc.at[h], cc.at[h], other).wait_recv()
+            kc[h] = ct[h, :, pl.ds(512, 512)] + cc[h]
+            for q in copies:
+                q.start()
+
+        away_sends.extend(copies)
+
+    mine = pl.ds(pl.multiple_of(wrap(x - y + 4) * 64, 64), 64)
+
+    pair = lax.div(z, 2)
+    b_slot = zl * 2 + c
+
+    def b_copies(h):
+        base = names("sbr", h, 0)
+        for k in (1, 2, 3):
+            names("sbr", h, k)
+        return [pltpu.make_async_remote_copy(
+            src_ref=sb.at[h], dst_ref=fb.at[h, :, lanes(b_slot, 128)], send_sem=ss.at[names("sbs", h, k)],
+            recv_sem=rs.at[base + b_slot], device_id=(x * 2 + pair, y * 4 + wrap(z + k)), device_id_type=MESH)
+            for k in range(4)]
+
+    def finish_b(h):
+        for f in ODD_FIRST:
+            remote(("xb", f, h), bx.at[h, f - 1], bx.at[h, f - 1], xid(f)).wait_recv()
+        sb[h] = (kb[h, mine, :] + bx[h, 0]) + (bx[h, 1] + bx[h, 2])
+        copies = b_copies(h)
+        for q in copies[1:]:
+            go(q)
+
+        @pl.when(home)
+        def _():
+            fb[h, :, lanes(b_slot, 128)] = sb[h]
+
+        @pl.when(jnp.logical_not(home))
+        def _():
+            copies[0].start()
+
+        away_sends.append(copies[0])
+
+    def finish_c(h):
+        for f in ODD_FIRST:
+            remote(("xc", f, h), cx.at[h, f - 1], cx.at[h, f - 1], xid(f)).wait_recv()
+        total = (kc[h, mine, :] + cx[h, 0]) + (cx[h, 1] + cx[h, 2])
+        copy = remote(("sc", h), sc.at[h], fc.at[h], swap_mate)
+
+        @pl.when(home)
+        def _():
+            fc[h] = total
+
+        @pl.when(jnp.logical_not(home))
+        def _():
+            sc[h] = total
+            copy.start()
+
+        away_sends.append(copy)
+
+    def final_b(h):
+        for k in range(4):
+            @pl.when(jnp.logical_not(jnp.logical_and(home, b_slot == k)))
+            def _():
+                ref = fb.at[h, :, pl.ds(k * 128, 128)]
+                remote(("sbr", h, k), ref, ref, other).wait_recv()
+
+        fbs = split(fb[h])
+        for cols in (first, second):
+            dt[h, :, cols] = dot3(fbs, (wh[cols, :], wl[cols, :]), NT)
+
+    def final_c(h):
+        @pl.when(jnp.logical_not(home))
+        def _():
+            remote(("sc", h), fc.at[h], fc.at[h], swap_mate).wait_recv()
+
+        dt[h] = fc[h] - dt[h]
+        for d in ODD_FIRST:
+            go(remote(("cy", d, h), dt.at[h, :, lanes(wrap(y + d), 128)], cy.at[h, d - 1], yid(d)))
+
+    def final(h):
+        final_b(h)
+        final_c(h)
+
+    def done(h):
+        for d in ODD_FIRST:
+            remote(("cy", d, h), cy.at[h, d - 1], cy.at[h, d - 1], yid(d)).wait_recv()
+        res = ((dt[h, :, lanes(y, 128)] + cy[h, 0]) + (cy[h, 1] + cy[h, 2])) / N
+        of[pl.ds(h * 32, 32), :] = res[:32]
+        of[pl.ds(128 + h * 32, 32), :] = res[32:]
+
+    split_block(mk, y, 0)
     for e in (1, 3, 2):
         arrived(part(y_m_in, d=4 - e))
         start(part(z_m, e=e))
-
-    @pl.loop(0, 8)
-    def _(i):
-        rows = pl.ds(pl.multiple_of(i * 64, 64), 64)
-        rh[rows, :], rl[rows, :] = split(mk[rows, :])
-
-    arrived(part(z_v_in, s=1, p=1), part(z_v_in, s=3, p=0), part(z_vf_in, s=1), part(z_vf_in, s=3))
+        split_block(mk, wrap(y + e), 0)
+    arrived(*[part(z_v_in, to="p", p=p) for p in (0, 1)], *[part(z_vf_in, p=p) for p in (0, 1)])
 
     @pl.loop(0, 8)
     def _(i):
@@ -282,19 +440,16 @@
         rows = pl.ds(pl.multiple_of(1024 + i * 64, 64), 64)
         rh[rows, :], rl[rows, :] = split(vk[p, yy].reshape(64, W))
 
-    first, second = pl.ds(0, 256), pl.ds(256, 256)
-
+    v1s, v2s = pl.ds(1024, 256), pl.ds(1280, 256)
+    gram = dot3((rh[v1s, :], rl[v1s, :]), (rh[v2s, :], rl[v2s, :]), NT)
+    at[:, pl.ds(32, 8), first] = gram[:128].reshape(16, 8, 256)
+    at[:, pl.ds(32, 8), second] = gram[128:].reshape(16, 8, 256)
     for t in (0, 1):
         rows = pl.ds(t * 256, 256)
         for j, cols in ((0, first), (1, second)):
             vrows = pl.ds(1024 + j * 256, 256)
             res = dot3((rh[rows, :], rl[rows, :]), (rh[vrows, :], rl[vrows, :]), NT)
             at[pl.ds(t * 8, 8), pl.ds(0, 32), cols] = res.reshape(8, 32, 256)
-
-    v1s, v2s = pl.ds(1024, 256), pl.ds(1280, 256)
-    gram = dot3((rh[v1s, :], rl[v1s, :]), (rh[v2s, :], rl[v2s, :]), NT)
-    at[:, pl.ds(32, 8), first] = gram[:128].reshape(16, 8, 256)
-    at[:, pl.ds(32, 8), second] = gram[128:].reshape(16, 8, 256)
 
     core_sum = go(remote(("ac",), at.at[pl.ds((1 - c) * 8, 8)], ac, other))
     z_panel(0)
@@ -313,151 +468,7 @@
     two = [go(remote(("ay", d), as_.at[0], ay.at[d - 1], yid(d))) for d in ODD_FIRST]
     two += [go(remote(("bx", d), as_.at[1], bx_.at[d - 1], xid(d))) for d in ODD_FIRST]
 
-    def product(h, lo, hi):
-        for t in range(lo, hi):
-            rows = pl.ds(t * 256, 256)
-            ct[h, :, rows] = dot3((ph[h], plo[h]), (rh[rows, :], rl[rows, :]), NT)
-
-    def landed(h):
-        arrived(*([part(z_pe_in, e=e, h=h) for e in (1, 3, 2)] if h == 3 else [part(z_p_in, h=h)]),
-                *([part(z_p0_in, k=0)] if h == 0 else [part(z_p0_in, k=1)] if h == 3 else []))
-
-        @pl.loop(0, 4)
-        def _(e):
-            rows = pl.ds(pl.multiple_of(e * 64, 64), 64)
-            ph[h, rows, :], plo[h, rows, :] = split(pk[h, e].reshape(64, W))
-
-    def early(h):
-        panel = pl.ds(pl.multiple_of(1024 + zl * 256, 256), 256)
-        bt[h] = dot3((ph[h], plo[h]), (rh[panel, :], rl[panel, :]), NT)
-        go(remote(("cb", h), bt.at[h, :, lanes(1 - c, 128)], cb.at[h], other))
-        product(h, 0, 2)
-        copy = remote(("cc", h), ct.at[h, :, pl.ds(0, 512)], cc.at[h], other)
-
-        @pl.when(jnp.logical_not(home))
-        def _():
-            copy.start()
-
-        away_sends.append(copy)
-
-    def along_x(name, h, src, dst):
-        out = []
-        for f in ODD_FIRST:
-            e = wrap(x + f - y + 4)
-            out.append(remote((name, f, h), src.at[h, pl.ds(pl.multiple_of(e * 64, 64), 64)], dst.at[h, f - 1], xid(f)))
-        return out
-
-    def early_x(h):
-        remote(("cb", h), cb.at[h], cb.at[h], other).wait_recv()
-        kb[h] = bt[h, :, lanes(c, 128)] + cb[h]
-        for q in along_x("xb", h, kb, bx):
-            go(q)
-        copies = along_x("xc", h, kc, cx)
-
-        @pl.when(home)
-        def _():
-            remote(("cc", h), cc.at[h], cc.at[h], other).wait_recv()
-            kc[h] = ct[h, :, pl.ds(0, 512)] + cc[h]
-            for q in copies:
-                q.start()
-
-        home_sends.extend(copies)
-
-    def late(h):
-        product(h, 2, 4)
-        copy = remote(("cc", h), ct.at[h, :, pl.ds(512, 512)], cc.at[h], other)
-
-        @pl.when(home)
-        def _():
-            copy.start()
-
-        home_sends.append(copy)
-
-    def late_x(h):
-        copies = along_x("xc", h, kc, cx)
-
-        @pl.when(jnp.logical_not(home))
-        def _():
-            remote(("cc", h), cc.at[h], cc.at[h], other).wait_recv()
-            kc[h] = ct[h, :, pl.ds(512, 512)] + cc[h]
-            for q in copies:
-                q.start()
-
-        away_sends.extend(copies)
-
-    mine = pl.ds(pl.multiple_of(wrap(x - y + 4) * 64, 64), 64)
-
-    pair = lax.div(z, 2)
-    b_slot = zl * 2 + c
-
-    def b_copies(h):
-        base = names("sbr", h, 0)
-        for k in (1, 2, 3):
-            names("sbr", h, k)
-        return [pltpu.make_async_remote_copy(
-            src_ref=sb.at[h], dst_ref=fb.at[h, :, lanes(b_slot, 128)], send_sem=ss.at[names("sbs", h, k)],
-            recv_sem=rs.at[base + b_slot], device_id=(x * 2 + pair, y * 4 + wrap(z + k)), device_id_type=MESH)
-            for k in range(4)]
-
-    def finish_b(h):
-        for f in ODD_FIRST:
-            remote(("xb", f, h), bx.at[h, f - 1], bx.at[h, f - 1], xid(f)).wait_recv()
-        sb[h] = (kb[h, mine, :] + bx[h, 0]) + (bx[h, 1] + bx[h, 2])
-        copies = b_copies(h)
-        for q in copies[1:]:
-            go(q)
-
-        @pl.when(home)
-        def _():
-            fb[h, :, lanes(b_slot, 128)] = sb[h]
-
-        @pl.when(jnp.logical_not(home))
-        def _():
-            copies[0].start()
-
-        away_sends.append(copies[0])
-
-    def finish_c(h):
-        for f in ODD_FIRST:
-            remote(("xc", f, h), cx.at[h, f - 1], cx.at[h, f - 1], xid(f)).wait_recv()
-        total = (kc[h, mine, :] + cx[h, 0]) + (cx[h, 1] + cx[h, 2])
-        copy = remote(("sc", h), sc.at[h], fc.at[h], swap_mate)
-
-        @pl.when(home)
-        def _():
-            fc[h] = total
-
-        @pl.when(jnp.logical_not(home))
-        def _():
-            sc[h] = total
-            copy.start()
-
-        away_sends.append(copy)
-
-    def final(h):
-        for k in range(4):
-            @pl.when(jnp.logical_not(jnp.logical_and(home, b_slot == k)))
-            def _():
-                ref = fb.at[h, :, pl.ds(k * 128, 128)]
-                remote(("sbr", h, k), ref, ref, other).wait_recv()
-
-        @pl.when(jnp.logical_not(home))
-        def _():
-            remote(("sc", h), fc.at[h], fc.at[h], swap_mate).wait_recv()
-
-        fbs = split(fb[h])
-        for cols in (first, second):
-            dt[h, :, cols] = fc[h, :, cols] - dot3(fbs, (wh[cols, :], wl[cols, :]), NT)
-        for d in ODD_FIRST:
-            go(remote(("cy", d, h), dt.at[h, :, lanes(wrap(y + d), 128)], cy.at[h, d - 1], yid(d)))
-
-    def done(h):
-        for d in ODD_FIRST:
-            remote(("cy", d, h), cy.at[h, d - 1], cy.at[h, d - 1], yid(d)).wait_recv()
-        res = ((dt[h, :, lanes(y, 128)] + cy[h, 0]) + (cy[h, 1] + cy[h, 2])) / N
-        of[pl.ds(h * 32, 32), :] = res[:32]
-        of[pl.ds(128 + h * 32, 32), :] = res[32:]
-
+    y_panel(3, (1, 3))
     landed(0)
     early(0)
     early_x(0)
@@ -469,10 +480,26 @@
     for d in ODD_FIRST:
         go(remote(("cx", d), af.at[a0 + x], af.at[a0 + x], xid(d)))
         go(remote(("dy", d), af.at[b0 + y], af.at[b0 + y], yid(d)))
-    y_panel(3)
+    y_panel(3, (2,))
     landed(1)
     early(1)
     early_x(1)
+
+    def modes_landed():
+        arrived(part(z_m0_in, k=0), part(z_m0_in, k=1))
+        split_block(mp, y, 512)
+        for e in (1, 3, 2):
+            rows = mrow(wrap(y + e))
+            both(lambda n: remote(("zm", e), mp.at[rows, pl.ds(0, n * 128)], mp.at[rows, pl.ds(0, n * 128)],
+                                  m_mate).wait_recv())
+            split_block(mp, wrap(y + e), 512)
+
+    def z_last(*es):
+        arrived(*[part(y_p_in, d=4 - e, h=3) for e in es])
+        start(*[part(z_pe, e=e, h=3) for e in es])
+
+    modes_landed()
+    late(0)
     for d in ODD_FIRST:
         ref = af.at[a0 + wrap(x + 4 - d)]
         remote(("cx", d), ref, ref, xid(d)).wait_recv()
@@ -480,18 +507,10 @@
         remote(("dy", d), ref, ref, yid(d)).wait_recv()
     ref = af.at[pl.ds(c * 8, 8)]
     go(remote(("bc",), ref, ref, other))
-    landed(2)
-    early(2)
+    late_x(0)
+    late(1)
     ref = af.at[pl.ds((1 - c) * 8, 8)]
     remote(("bc",), ref, ref, other).wait_recv()
-
-
-    early_x(2)
-
-    def z_last(*es):
-        arrived(*[part(y_p_in, d=4 - e, h=3) for e in es])
-        start(*[part(z_pe, e=e, h=3) for e in es])
-
     z_last(1, 3)
 
     gram = jnp.concatenate([af[:, pl.ds(32, 8), first].reshape(128, 256),
@@ -517,34 +536,20 @@
     def own_r(n):
         return pltpu.make_async_copy(mv.at[mrow(y), pl.ds(0, n * 128)], out_m.at[:, quarter(y, n)], ls.at[4])
 
-    def modes_landed():
-        arrived(part(z_m0_in, k=0), part(z_m0_in, k=1))
-        for e in (1, 3, 2):
-            rows = mrow(wrap(y + e))
-            both(lambda n: remote(("zm", e), mp.at[rows, pl.ds(0, n * 128)], mp.at[rows, pl.ds(0, n * 128)],
-                                  m_mate).wait_recv())
-
-        @pl.loop(0, 8)
-        def _(i):
-            rows = pl.ds(pl.multiple_of(i * 64, 64), 64)
-            to = pl.ds(pl.multiple_of(512 + i * 64, 64), 64)
-            rh[to, :], rl[to, :] = split(mp[rows, :])
-
+    late_x(1)
     move(1)
     start(part(y_r, d=1, half=0))
     move(3)
     start(part(y_r, d=3, half=0))
     z_last(2)
-    modes_landed()
-    late(0)
+    landed(2)
+    early(2)
     move(2)
     start(part(y_r, d=2, half=0))
-    late_x(0)
+    early_x(2)
+    late(2)
     move(0)
     both(lambda n: own_r(n).start())
-    late(1)
-    late(2)
-    late_x(1)
     late_x(2)
     start(*[part(y_r, d=d, half=1) for d in ODD_FIRST])
     finish_b(0)
@@ -563,10 +568,11 @@
     finish_b(3)
     finish_c(3)
     final(2)
+    final_b(3)
+    final_c(3)
+    drain()
     done(0)
     done(1)
-    final(3)
-    drain()
     done(2)
     done(3)
     out_c[...] = of[...].T

time: 115 us -> 110 us (0.957)
  Pallas kernels: 110 us -> 106 us
    pallas_call x1, Pallas kernels: 110 us -> 106 us  [shards(): pl.pallas_call(kernel, out_shape=(jax.ShapeDtypeStruct((128, 3840), F32),...]
where the time goes in v4:
time: 110 us
  Pallas kernels  106 us (96%)
  local copies, waits for them, and re-layouts  3.64 us (3%)
    pallas_call x1, Pallas kernels, shards(): pl.pallas_call(kernel, out_shape=(jax.ShapeDtypeStruct((128, 3840), F32),...  106 us
    unnamed x4, local copies, waits for them, and re-layouts  3.64 us

profile of v4, /device:TPU:1, one launch (start us, length us, event | category | flops | bytes accessed | tf_op | source)
XLA Modules:
  0.0 110.0 jit_solution(8795067336651532733)
XLA Ops:
  0.6 105.7 %reflect_and_correlate.1 = (f32[128,3840]{1,0:T(8,128)}, f32[128,256]{1,0:T(8,128)}) custom-call(f32[128,3840]{1,0:T(8,128)} %m_in.1, f32[4,32,3840]{2,1,0:T(8,128)} %bitcast.1, f32[16,3840]{1,0:T(8,128)} %v1_in.1, f32[16,3840]{1,0:T(8,128)} %v2_in.1, f32[256,256]{1,0:T(8,128)} %f1.1, f32[256,256]{1,0:T(8,128)} %f2.1), custom_call_target="tpu_custom_call" | custom-call | tf_op jit(solution)/shard_map/reflect_and_correlate/pallas_call | solution.py:592
  106.4 0.0 copy-start
  106.4 3.0 %copy.10 = f32[128,3840]{1,0:T(8,128)} copy(f32[128,3840]{1,0:T(8,128)} %get-tuple-element.4) | data formatting | bytes 3932160
  109.4 0.0 copy-done
  109.4 0.7 copy.11
Async XLA Ops:
  106.4 3.0 %copy-start = (f32[128,256]{1,0:T(8,128)S(1)}, f32[128,256]{1,0:T(8,128)}, u32[]{:S(2)}) copy-start(f32[128,256]{1,0:T(8,128)} %get-tuple-element.5) | copy-start | bytes 393220

commit v5 on v4

--- a/solution.py
+++ b/solution.py
@@ -40,7 +40,7 @@
 
 def kernel(m_in, p_in, v1_in, v2_in, f1, f2, out_m, out_c,
            mk, mp, mv, pk, vk, rh, rl, ph, plo, at, ac, ax, ay, bx_, by_, as_, af, wh, wl,
-           ct, bt, cc, cb, kc, kb, cx, bx, sc, sb, fc, fb, dt, cy, of, ss, rs, ls):
+           ct, bt, cc, cb, kc, kb, cx, bx, sc, sb, fc, fb, dt, cy, ss, rs, ls):
     r, col = lax.axis_index("row"), lax.axis_index("col")
     x, c = lax.div(r, 2), lax.rem(r, 2)
     y, z = lax.div(col, 4), lax.rem(col, 4)
@@ -424,8 +424,8 @@
         for d in ODD_FIRST:
             remote(("cy", d, h), cy.at[h, d - 1], cy.at[h, d - 1], yid(d)).wait_recv()
         res = ((dt[h, :, lanes(y, 128)] + cy[h, 0]) + (cy[h, 1] + cy[h, 2])) / N
-        of[pl.ds(h * 32, 32), :] = res[:32]
-        of[pl.ds(128 + h * 32, 32), :] = res[32:]
+        out_c[pl.ds(h * 32, 32), :] = res[:32]
+        out_c[pl.ds(128 + h * 32, 32), :] = res[32:]
 
     split_block(mk, y, 0)
     for e in (1, 3, 2):
@@ -575,7 +575,6 @@
     done(1)
     done(2)
     done(3)
-    out_c[...] = of[...].T
 
     arrived(*[part(y_r_in, d=d, half=half) for half in (0, 1) for d in ODD_FIRST])
     both(lambda n: own_r(n).wait())
@@ -583,15 +582,33 @@
 
 
 SEMS = 192
+
+
+def place(m_ref, t_ref, m_out, c_out, m_buf, t_buf, c_buf, come, go):
+    rows = [pl.ds(i * 16, 16) for i in range(8)]
+    reads = [pltpu.make_async_copy(t_ref, t_buf, come.at[8])]
+    reads += [pltpu.make_async_copy(m_ref.at[q], m_buf.at[q], come.at[i]) for i, q in enumerate(rows)]
+    writes = [pltpu.make_async_copy(c_buf, c_out, go.at[8])]
+    writes += [pltpu.make_async_copy(m_buf.at[q], m_out.at[q], go.at[i]) for i, q in enumerate(rows)]
+    for copy in reads:
+        copy.start()
+    reads[0].wait()
+    c_buf[...] = t_buf[...].T
+    writes[0].start()
+    for come_in, go_out in zip(reads[1:], writes[1:]):
+        come_in.wait()
+        go_out.start()
+    for copy in writes:
+        copy.wait()
 
 
 def shards(modes, prev_modes, first_vectors, first_factor, second_vectors, second_factor):
     any_, vmem = pl.BlockSpec(memory_space=pl.ANY), pl.BlockSpec(memory_space=pltpu.VMEM)
     V = pltpu.VMEM
     dma = pltpu.SemaphoreType.DMA
-    return pl.pallas_call(
+    moved, turned = pl.pallas_call(
         kernel,
-        out_shape=(jax.ShapeDtypeStruct((128, 3840), F32), jax.ShapeDtypeStruct((128, 256), F32)),
+        out_shape=(jax.ShapeDtypeStruct((128, 3840), F32), jax.ShapeDtypeStruct((256, 128), F32)),
         in_specs=[any_, any_, any_, any_, vmem, vmem],
         out_specs=(any_, vmem),
         scratch_shapes=[
@@ -603,13 +620,22 @@
             V((4, 256, 1024), F32), V((4, 256, 256), F32), V((4, 256, 512), F32), V((4, 256, 128), F32),
             V((4, 256, 512), F32), V((4, 256, 128), F32), V((4, 3, 64, 512), F32), V((4, 3, 64, 128), F32),
             V((4, 64, 512), F32), V((4, 64, 128), F32), V((4, 64, 512), F32), V((4, 64, 512), F32),
-            V((4, 64, 512), F32), V((4, 3, 64, 128), F32), V((256, 128), F32),
+            V((4, 64, 512), F32), V((4, 3, 64, 128), F32),
             dma((SEMS,)), dma((SEMS,)), dma((5,)),
         ],
         compiler_params=pltpu.CompilerParams(
             collective_id=0, has_side_effects=True, vmem_limit_bytes=60 * 2**20),
         name="reflect_and_correlate",
     )(modes, prev_modes.reshape(4, 32, 3840), first_vectors, second_vectors, first_factor, second_factor)
+    return pl.pallas_call(
+        place,
+        out_shape=(jax.ShapeDtypeStruct((128, 3840), F32), jax.ShapeDtypeStruct((128, 256), F32)),
+        in_specs=[any_, any_],
+        out_specs=(any_, any_),
+        scratch_shapes=[V((128, 3840), F32), V((256, 128), F32), V((128, 256), F32), dma((9,)), dma((9,))],
+        compiler_params=pltpu.CompilerParams(vmem_limit_bytes=60 * 2**20),
+        name="place",
+    )(moved, turned)
 
 
 def solution(mesh):

time: 110 us -> 109 us (level)
  local copies, waits for them, and re-layouts: 3.64 us -> 0 us
  Pallas kernels: 106 us -> 108 us
    unnamed x4 -> x0, local copies, waits for them, and re-layouts: 3.64 us -> none
    pallas_call x0 -> x1, Pallas kernels: none -> 2.51 us  [shards(): pl.pallas_call(place, out_shape=(jax.ShapeDtypeStruct((128, 3840), F32),...]
where the time goes in v5:
time: 109 us
  Pallas kernels  108 us (99%)
    pallas_call x1, Pallas kernels, shards(): pl.pallas_call(kernel, out_shape=(jax.ShapeDtypeStruct((128, 3840), F32),...  106 us
    pallas_call x1, Pallas kernels, shards(): pl.pallas_call(place, out_shape=(jax.ShapeDtypeStruct((128, 3840), F32),...  2.51 us

profile of v5, /device:TPU:1, one launch (start us, length us, event | category | flops | bytes accessed | tf_op | source)
XLA Modules:
  0.0 109.0 jit_solution(7471766199120244982)
XLA Ops:
  0.6 105.7 %reflect_and_correlate.1 = (f32[128,3840]{1,0:T(8,128)}, f32[256,128]{1,0:T(8,128)}) custom-call(f32[128,3840]{1,0:T(8,128)} %m_in.1, f32[4,32,3840]{2,1,0:T(8,128)} %bitcast.1, f32[16,3840]{1,0:T(8,128)} %v1_in.1, f32[16,3840]{1,0:T(8,128)} %v2_in.1, f32[256,256]{1,0:T(8,128)} %f1.1, f32[256,256]{1,0:T(8,128)} %f2.1), custom_call_target="tpu_custom_call" | custom-call | tf_op jit(solution)/shard_map/reflect_and_correlate/pallas_call | solution.py:609
  106.3 2.5 %place.1 = (f32[128,3840]{1,0:T(8,128)}, f32[128,256]{1,0:T(8,128)}) custom-call(f32[128,3840]{1,0:T(8,128)} %get-tuple-element.4.m_ref, f32[256,128]{1,0:T(8,128)} %get-tuple-element.5.t_ref), custom_call_target="tpu_custom_call" | custom-call | tf_op jit(solution)/shard_map/place/pallas_call | solution.py:630

commit v6 on v5

--- a/solution.py
+++ b/solution.py
@@ -498,6 +498,7 @@
         arrived(*[part(y_p_in, d=4 - e, h=3) for e in es])
         start(*[part(z_pe, e=e, h=3) for e in es])
 
+    z_last(1, 3)
     modes_landed()
     late(0)
     for d in ODD_FIRST:
@@ -511,7 +512,6 @@
     late(1)
     ref = af.at[pl.ds((1 - c) * 8, 8)]
     remote(("bc",), ref, ref, other).wait_recv()
-    z_last(1, 3)
 
     gram = jnp.concatenate([af[:, pl.ds(32, 8), first].reshape(128, 256),
                             af[:, pl.ds(32, 8), second].reshape(128, 256)], axis=0)
@@ -536,12 +536,12 @@
     def own_r(n):
         return pltpu.make_async_copy(mv.at[mrow(y), pl.ds(0, n * 128)], out_m.at[:, quarter(y, n)], ls.at[4])
 
+    z_last(2)
     late_x(1)
     move(1)
     start(part(y_r, d=1, half=0))
     move(3)
     start(part(y_r, d=3, half=0))
-    z_last(2)
     landed(2)
     early(2)
     move(2)

time: 109 us -> 109 us (level)
  no operation moved by 1% of the time
where the time goes in v6:
time: 109 us
  Pallas kernels  108 us (99%)
    pallas_call x1, Pallas kernels, shards(): pl.pallas_call(kernel, out_shape=(jax.ShapeDtypeStruct((128, 3840), F32),...  106 us
    pallas_call x1, Pallas kernels, shards(): pl.pallas_call(place, out_shape=(jax.ShapeDtypeStruct((128, 3840), F32),...  2.51 us

profile of v6, /device:TPU:1, one launch (start us, length us, event | category | flops | bytes accessed | tf_op | source)
XLA Modules:
  0.0 108.9 jit_solution(3110330756952409213)
XLA Ops:
  0.6 105.6 %reflect_and_correlate.1 = (f32[128,3840]{1,0:T(8,128)}, f32[256,128]{1,0:T(8,128)}) custom-call(f32[128,3840]{1,0:T(8,128)} %m_in.1, f32[4,32,3840]{2,1,0:T(8,128)} %bitcast.1, f32[16,3840]{1,0:T(8,128)} %v1_in.1, f32[16,3840]{1,0:T(8,128)} %v2_in.1, f32[256,256]{1,0:T(8,128)} %f1.1, f32[256,256]{1,0:T(8,128)} %f2.1), custom_call_target="tpu_custom_call" | custom-call | tf_op jit(solution)/shard_map/reflect_and_correlate/pallas_call | solution.py:609
  106.2 2.5 %place.1 = (f32[128,3840]{1,0:T(8,128)}, f32[128,256]{1,0:T(8,128)}) custom-call(f32[128,3840]{1,0:T(8,128)} %get-tuple-element.4.m_ref, f32[256,128]{1,0:T(8,128)} %get-tuple-element.5.t_ref), custom_call_target="tpu_custom_call" | custom-call | tf_op jit(solution)/shard_map/place/pallas_call | solution.py:630
